TPU v7x, 32 devices: a whole 2x2x4 slice. The times are simulated.
32 devices in a mesh: chan: 8 (over y, x, core), tm: 4 (over z).
Axes of the slice: x: 2, y: 2, z: 4, core: 2. Of those that a mesh axis runs over, the one named last changes fastest.
Arguments:
- record: bfloat16 [10240, 16384], P('chan', 'tm'), may hold values from -6 to 6
- channel_ok: int32 [10240], P('chan'), may hold values 0 or 1
- fan_bounds: int32 [2, 8193], replicated, may hold values from 0 to 5120, as said below
Outputs:
- slowness: float32 [10240, 16384], P('chan', 'tm')
Inputs may be any that keep to these rules, and one draw needn't show every extreme that they name: fan_bounds[0, g] <= fan_bounds[1, g] for every g; fan_bounds[0, 0] is 0 and fan_bounds[1, 8192] is 5120.
All inputs are finite; a program needn't handle non-finite values. No bound on the sum of `channel_ok` on one device may be relied on, other than what follows from the above.
Results may differ from a plain program's by a relative error of at most 0.0063.
Values may be sent and summed in bfloat16 or wider, within the bound.
A program may use at most 192 MiB of HBM per device.

v0:
```python
import math

import jax
import jax.numpy as jnp
from jax import lax
from jax.sharding import PartitionSpec as P

NC = 10240
NT = 16384
TF = 128
R = 4


def padded_2(cells, sides, width):
    for axis, dim in sides:
        count = lax.axis_size(axis)
        ends = count - 1
        head = lax.slice_in_dim(cells, 0, width, axis=dim)
        tail = lax.slice_in_dim(cells, cells.shape[dim] - width, cells.shape[dim], axis=dim)
        cells = jnp.concatenate(
            [
                lax.ppermute(tail, axis, [(i, (i + 1) % count) for i in range(ends)]),
                cells,
                lax.ppermute(head, axis, [((i + 1) % count, i) for i in range(ends)]),
            ],
            axis=dim,
        )
    return cells


def contract(pattern, left_arg, right_arg):
    return jnp.einsum(
        pattern,
        left_arg,
        right_arg,
        precision=lax.Precision.HIGH,
        preferred_element_type=jnp.float32,
    )


def rotations(row_digits, col_digits, length):
    phase_int = row_digits[:, None] * col_digits[None, :] % length
    angles = phase_int.astype(jnp.float32) * (2.0 * math.pi / length)
    return (jnp.cos(angles), jnp.sin(angles))


def time_forward(samples, keep):
    row_count = samples.shape[0]
    signal = samples.astype(jnp.float32).reshape(row_count, TF, TF)
    digits = jnp.arange(TF, dtype=jnp.int32)
    cos_w, sin_w = rotations(digits, digits, TF)
    tw_cos, tw_sin = rotations(digits, digits, TF * TF)
    first_re = contract("rmn,km->rkn", signal, cos_w)
    first_im = -contract("rmn,km->rkn", signal, sin_w)
    turned_re = first_re * tw_cos + first_im * tw_sin
    turned_im = first_im * tw_cos - first_re * tw_sin
    cos_k = cos_w[:keep]
    sin_k = sin_w[:keep]
    spec_re = contract("rkn,jn->rkj", turned_re, cos_k) + contract("rkn,jn->rkj", turned_im, sin_k)
    spec_im = contract("rkn,jn->rkj", turned_im, cos_k) - contract("rkn,jn->rkj", turned_re, sin_k)
    highest = contract("rn,n->r", turned_re[:, 0, :], cos_w[TF // 2])
    spec_im = spec_im.at[:, 0, 0].set(highest)
    return (
        spec_re.reshape(row_count, TF * keep).astype(jnp.bfloat16),
        spec_im.reshape(row_count, TF * keep).astype(jnp.bfloat16),
    )


def time_inverse(back_re, back_im):
    row_count = back_re.shape[0]
    part_re = back_re.astype(jnp.float32).reshape(row_count, TF, TF)
    part_im = back_im.astype(jnp.float32).reshape(row_count, TF, TF)
    digits = jnp.arange(TF, dtype=jnp.int32)
    cos_w, sin_w = rotations(digits, digits, TF)
    tw_cos, tw_sin = rotations(digits, digits, TF * TF)
    mixed_re = contract("rkj,jn->rkn", part_re, cos_w) - contract("rkj,jn->rkn", part_im, sin_w)
    mixed_im = contract("rkj,jn->rkn", part_im, cos_w) + contract("rkj,jn->rkn", part_re, sin_w)
    turned_re = mixed_re * tw_cos - mixed_im * tw_sin
    turned_im = mixed_im * tw_cos + mixed_re * tw_sin
    result = contract("rkn,km->rmn", turned_re, cos_w) - contract("rkn,km->rmn", turned_im, sin_w)
    return (result / NT).reshape(row_count, NT).astype(jnp.bfloat16)


def unfold_half(half_re, half_im):
    row_count = half_re.shape[0]
    width = TF // 2
    lower_re = half_re.reshape(row_count, TF, width)
    lower_im = half_im.reshape(row_count, TF, width)
    highest = lower_re[:, 0, 0:1] * 0 + lower_im[:, 0, 0:1]
    lower_im = lower_im.at[:, 0, 0].set(jnp.zeros((row_count,), jnp.bfloat16))
    rest_re = jnp.flip(jnp.flip(lower_re[:, 1:, :], 1), 2)
    rest_im = -jnp.flip(jnp.flip(lower_im[:, 1:, :], 1), 2)
    first_re = jnp.concatenate([highest, jnp.flip(lower_re[:, 0, 1:], 1)], axis=1)
    first_im = jnp.concatenate(
        [jnp.zeros((row_count, 1), jnp.bfloat16), -jnp.flip(lower_im[:, 0, 1:], 1)], axis=1
    )
    upper_re = jnp.concatenate([first_re[:, None, :], rest_re], axis=1)
    upper_im = jnp.concatenate([first_im[:, None, :], rest_im], axis=1)
    full_re = jnp.concatenate([lower_re, upper_re], axis=2).reshape(row_count, NT)
    full_im = jnp.concatenate([lower_im, upper_im], axis=2).reshape(row_count, NT)
    return (full_re, full_im)


def reversed_waves(values):
    along_outer = jnp.roll(jnp.flip(values, 0), 1, axis=0)
    along_inner = jnp.flip(along_outer, 1)
    first_row = jnp.roll(along_inner[0:1], 1, axis=1)
    return jnp.concatenate([first_row, along_inner[1:]], axis=0)


def channel_filter(
    pencil_re, pencil_im, position, lower_bound, upper_bound, top_low, top_high, packed
):
    devices = position.shape[0]
    row_depth = NC // devices
    columns = pencil_re.shape[1]
    part_re = pencil_re.astype(jnp.float32).reshape(devices, row_depth, columns)
    part_im = pencil_im.astype(jnp.float32).reshape(devices, row_depth, columns)
    outer_digits = jnp.arange(devices, dtype=jnp.int32)
    inner_digits = jnp.arange(row_depth, dtype=jnp.int32)
    cos_a, sin_a = rotations(outer_digits, position, devices)
    cos_b, sin_b = rotations(inner_digits, inner_digits, row_depth)
    tw_cos, tw_sin = rotations(outer_digits, inner_digits, NC)
    tw_cos = tw_cos[:, :, None]
    tw_sin = tw_sin[:, :, None]
    first_re = contract("pbf,kp->kbf", part_re, cos_a) + contract("pbf,kp->kbf", part_im, sin_a)
    first_im = contract("pbf,kp->kbf", part_im, cos_a) - contract("pbf,kp->kbf", part_re, sin_a)
    turned_re = first_re * tw_cos + first_im * tw_sin
    turned_im = first_im * tw_cos - first_re * tw_sin
    wave_re = contract("kbf,jb->kjf", turned_re, cos_b) + contract("kbf,jb->kjf", turned_im, sin_b)
    wave_im = contract("kbf,jb->kjf", turned_im, cos_b) - contract("kbf,jb->kjf", turned_re, sin_b)
    number = outer_digits[:, None] + devices * inner_digits[None, :]
    folded = jnp.minimum(number, NC - number)
    passing = (
        (folded[:, :, None] >= lower_bound[None, None, :])
        & (folded[:, :, None] <= upper_bound[None, None, :])
    ).astype(jnp.float32)
    top_pass = ((folded >= top_low) & (folded <= top_high)).astype(jnp.float32)
    first_pass = passing[:, :, 0]
    column_re = wave_re[:, :, 0]
    column_im = wave_im[:, :, 0]
    mirror_re = reversed_waves(column_re)
    mirror_im = reversed_waves(column_im)
    even_part = (first_pass + top_pass) * 0.5
    odd_part = (first_pass - top_pass) * 0.5
    split_re = even_part * column_re + odd_part * mirror_re
    split_im = even_part * column_im - odd_part * mirror_im
    wave_re = wave_re * passing
    wave_im = wave_im * passing
    wave_re = wave_re.at[:, :, 0].set(packed * split_re + (1.0 - packed) * wave_re[:, :, 0])
    wave_im = wave_im.at[:, :, 0].set(packed * split_im + (1.0 - packed) * wave_im[:, :, 0])
    back_re = contract("kjf,jb->kbf", wave_re, cos_b) - contract("kjf,jb->kbf", wave_im, sin_b)
    back_im = contract("kjf,jb->kbf", wave_im, cos_b) + contract("kjf,jb->kbf", wave_re, sin_b)
    untwist_re = back_re * tw_cos - back_im * tw_sin
    untwist_im = back_im * tw_cos + back_re * tw_sin
    out_re = contract("kbf,kp->pbf", untwist_re, cos_a) - contract("kbf,kp->pbf", untwist_im, sin_a)
    out_im = contract("kbf,kp->pbf", untwist_im, cos_a) + contract("kbf,kp->pbf", untwist_re, sin_a)
    return (
        (out_re / NC).reshape(NC, columns).astype(jnp.bfloat16),
        (out_im / NC).reshape(NC, columns).astype(jnp.bfloat16),
    )


def box_sum(values, dim_index, radius):
    length = values.shape[dim_index] - 2 * radius
    running = lax.slice_in_dim(values, 0, length, axis=dim_index)
    for offset in range(1, 2 * radius + 1):
        running = running + lax.slice_in_dim(values, offset, offset + length, axis=dim_index)
    return running


def gradients(padded):
    grad_chan = (padded[2:, 1:-1] - padded[:-2, 1:-1]) * 0.5
    grad_time = (padded[1:-1, 2:] - padded[1:-1, :-2]) * 0.5
    return (grad_chan, grad_time)


def per_device(record, channel_ok, fan_bounds):
    chan_count = lax.axis_size("chan")
    time_count = lax.axis_size("tm")
    devices = chan_count * time_count
    tile_chan, tile_time = record.shape
    radius = R
    tiles = record * channel_ok.astype(jnp.bfloat16)[:, None]
    series = lax.all_to_all(tiles, "tm", split_axis=0, concat_axis=1, tiled=True)
    block_index = lax.axis_index("chan") * time_count + lax.axis_index("tm")
    top_low = fan_bounds[0, NT // 2]
    top_high = fan_bounds[1, NT // 2]
    spec_re, spec_im = time_forward(series, TF // 2)
    columns = NT // (2 * devices)
    ordered = (
        fan_bounds[:, : NT // 2].reshape(2, TF // 2, TF).transpose(0, 2, 1).reshape(2, NT // 2)
    )
    packed = (block_index == 0).astype(jnp.float32)
    window = lax.dynamic_slice_in_dim(ordered, block_index * columns, columns, 1)
    slot_index = jnp.arange(devices, dtype=jnp.int32)
    pencil_re, pencil_im = (
        lax.all_to_all(spec_re, ("chan", "tm"), split_axis=1, concat_axis=0, tiled=True),
        lax.all_to_all(spec_im, ("chan", "tm"), split_axis=1, concat_axis=0, tiled=True),
    )
    filt_re, filt_im = channel_filter(
        pencil_re, pencil_im, slot_index, window[0], window[1], top_low, top_high, packed
    )
    back_re, back_im = (
        lax.all_to_all(filt_re, ("chan", "tm"), split_axis=0, concat_axis=1, tiled=True),
        lax.all_to_all(filt_im, ("chan", "tm"), split_axis=0, concat_axis=1, tiled=True),
    )
    back_re, back_im = unfold_half(back_re, back_im)
    filtered_rows = time_inverse(back_re, back_im)
    filtered = lax.all_to_all(filtered_rows, "tm", split_axis=1, concat_axis=0, tiled=True)
    padded = padded_2(filtered, (("chan", 0), ("tm", 1)), radius + 1).astype(jnp.float32)
    grad_chan, grad_time = gradients(padded)
    chan_pos = (
        lax.axis_index("chan") * tile_chan
        - radius
        + jnp.arange(tile_chan + 2 * radius, dtype=jnp.int32)
    )
    time_pos = (
        lax.axis_index("tm") * tile_time
        - radius
        + jnp.arange(tile_time + 2 * radius, dtype=jnp.int32)
    )
    chan_in = (chan_pos >= 0) & (chan_pos < NC)
    time_in = (time_pos >= 0) & (time_pos < NT)
    weight = (chan_in[:, None] & time_in[None, :]).astype(jnp.float32)
    products = jnp.stack([grad_chan * grad_time * weight, grad_time * grad_time * weight])
    summed = box_sum(box_sum(products, 1, radius), 2, radius)
    window_area = (2 * radius + 1) * (2 * radius + 1)
    cross_mean = summed[0] / window_area
    along_mean = summed[1] / window_area
    return -cross_mean / (along_mean + 1e-05)


def solution(mesh):
    in_specs = (P("chan", "tm"), P("chan"), P())
    out_specs = P("chan", "tm")
    return jax.shard_map(
        per_device, mesh=mesh, in_specs=in_specs, out_specs=out_specs, check_vma=False
    )
```

profile of v0, /device:TPU:19, one launch (start us, length us, event | category | flops | bytes accessed | tf_op | source)
XLA Modules:
  0.0 2539.9 jit_solution(12736872057830965090)
XLA Ops:
  17.5 223.6 %all-to-all-done = bf16[4,320,4096]{2,1,0:T(8,128)(2,1)} async-done(((bf16[4,320,4096]{2,1,0:T(8,128)(2,1)}), bf16[4,320,4096]{2,1,0:T(8,128)(2,1)}, u32[]{:S(2)}, u32[]{:S(2)}) %all-to-all-start) | async-done | bytes 10485792 | tf_op jit(solution)/shard_map/all_to_all | solution.py:185
  241.1 14.6 copy.256
  255.7 19.4 reshape.358
  284.8 18.8 fusion.137
  303.7 17.5 add_bitcast_fusion
  321.1 23.3 fusion.27
  344.4 18.0 add_convert_fusion
  390.6 23.1 fusion.25
  413.8 18.1 convolution_subtract_fusion
  456.7 47.2 %all-to-all-done.1 = bf16[320,32,256]{2,0,1:T(8,128)(2,1)} async-done(((bf16[320,32,256]{2,0,1:T(8,128)(2,1)}), bf16[320,32,256]{2,0,1:T(8,128)(2,1)}, u32[]{:S(2)}, u32[]{:S(2)}) %all-to-all-start.1) | async-done | bytes 5242912 | tf_op jit(solution)/shard_map/all_to_all | solution.py:198
  536.1 89.1 %all-to-all-done.2 = bf16[320,32,256]{2,0,1:T(8,128)(2,1)} async-done(((bf16[320,32,256]{2,0,1:T(8,128)(2,1)}), bf16[320,32,256]{2,0,1:T(8,128)(2,1)}, u32[]{:S(2)}, u32[]{:S(2)}) %all-to-all-start.2) | async-done | bytes 5242912 | tf_op jit(solution)/shard_map/all_to_all | solution.py:199
  635.3 21.4 multiply_add_fusion
  656.7 22.9 fusion.46
  679.6 18.7 fusion.44
  698.3 18.8 fusion.50
  717.2 18.6 fusion.48
  784.0 33.3 %broadcast_select_fusion.1 = (f32[32,320,256]{1,0,2:T(8,128)}, f32[32,320,256]{1,0,2:T(8,128)}, f32[32,320,256]{1,0,2:T(8,128)}, f32[32,320,256]{1,0,2:T(8,128)}) fusion(s32[256]{0:T(256)S(1)} %bitcast.210, s32[256]{0:T(256)S(1)} %bitcast.208, s32[32,320]{1,0:T(8,128)S(1)} %subtract_minimum_fusion.1, f32[320,32,256]{0,1,2:T(8,128)} %copy.274, ...), kind=kLoop, calls=%fused_computation.107 | loop fusion | flops 18350080 | bytes 83929088 | tf_op jit(solution)/shard_map/mul | solution.py:148
  839.0 17.9 fusion.75
  856.9 15.7 fusion.80
  884.7 18.2 fusion.73
  902.9 15.6 fusion.82
  918.6 39.2 %fusion.38 = (f32[32,320,256]{2,0,1:T(8,128)S(1)}, f32[32,320,256]{2,0,1:T(8,128)}) fusion(f32[32,320]{0,1:T(8,128)S(1)} %copy.269, f32[32,320]{0,1:T(8,128)S(1)} %copy.266, f32[320,32,256]{2,0,1:T(8,128)S(1)} %bitcast.195, f32[320,32,256]{2,0,1:T(8,128)} %fusion.82, f32[320,32,256]{2,0,1:T(8,128)} %fusion.73, f32[320,32,256]{2,0,1:T(8,128)} %fusion.80), kind=kLoop, calls=%fused_computation.79 | loop fusion | flops 20971520 | bytes 62996480 | tf_op jit(solution)/shard_map/sub | solution.py:154
  965.6 12.3 multiply_convert_fusion.2
  989.0 12.7 fusion.195
  1019.6 84.6 %all-to-all-done.3 = bf16[32,320,256]{2,1,0:T(8,128)(2,1)} async-done(((bf16[32,320,256]{2,1,0:T(8,128)(2,1)}), bf16[32,320,256]{2,1,0:T(8,128)(2,1)}, u32[]{:S(2)}, u32[]{:S(2)}) %all-to-all-start.3) | async-done | bytes 5242912 | tf_op jit(solution)/shard_map/all_to_all | solution.py:205
  1117.9 18.2 copy.300
  1136.1 89.1 %all-to-all-done.4 = bf16[32,320,256]{2,1,0:T(8,128)(2,1)} async-done(((bf16[32,320,256]{2,1,0:T(8,128)(2,1)}), bf16[32,320,256]{2,1,0:T(8,128)(2,1)}, u32[]{:S(2)}, u32[]{:S(2)}) %all-to-all-start.4) | async-done | bytes 5242912 | tf_op jit(solution)/shard_map/all_to_all | solution.py:206
  1233.3 18.2 copy.297
  1261.5 16.0 slice.386
  1279.6 16.1 slice.384
  1296.1 159.0 %rev.24 = bf16[320,127,64]{2,1,0:T(8,128)(2,1)} reverse(bf16[320,127,64]{2,1,0:T(8,128)(2,1)} %slice.384), dimensions={1,2} | reverse | bytes 10403840 | tf_op jit(solution)/shard_map/jit(_flip)/rev | solution.py:91
  1455.1 17.5 fusion.135
  1472.6 17.6 fusion.127
  1490.2 159.1 %rev.26 = bf16[320,127,64]{2,1,0:T(8,128)(2,1)} reverse(bf16[320,127,64]{2,1,0:T(8,128)(2,1)} %slice.386), dimensions={1,2} | reverse | bytes 10403840 | tf_op jit(solution)/shard_map/jit(_flip)/rev | solution.py:92
  1649.3 12.9 neg.16
  1662.7 17.7 fusion.129
  1680.4 17.7 fusion.133
  1698.2 37.0 %fusion.29 = f32[128,320,128]{2,0,1:T(8,128)} fusion(f32[128,128]{1,0:T(8,128)S(1)} %copy-done.5, f32[128,128]{1,0:T(8,128)S(1)} %copy-done.7, f32[320,128,128]{2,1,0:T(8,128)} %fusion.133, f32[320,128,128]{2,1,0:T(8,128)} %fusion.127, f32[320,128,128]{2,1,0:T(8,128)} %fusion.135, f32[320,128,128]{2,1,0:T(8,128)} %fusion.129), kind=kOutput, calls=%fused_computation.61 | convolution fusion | flops 4052975616 | bytes 104988672 | tf_op jit(solution)/shard_map/rkn,km->rmn/dot_general | solution.py:32
  1735.2 38.4 %fusion.37 = bf16[320,128,128]{2,1,0:T(8,128)(2,1)} fusion(f32[128,320,128]{2,0,1:T(8,128)} %fusion.29, f32[128,128]{1,0:T(8,128)S(1)} %copy-done.5, f32[128,128]{1,0:T(8,128)S(1)} %copy-done.7, f32[320,128,128]{2,1,0:T(8,128)} %fusion.133, f32[320,128,128]{2,1,0:T(8,128)} %fusion.127, f32[320,128,128]{2,1,0:T(8,128)} %fusion.135, f32[320,128,128]{2,1,0:T(8,128)} %fusion.129), kind=kOutput, calls=%fused_computation.74 | convolution fusion | flops 4068704256 | bytes 115474432 | tf_op jit(solution)/shard_map/rkn,km->rmn/dot_general | solution.py:32
  1773.6 15.4 convert_element_type.184
  1789.0 13.8 copy.306
  1809.4 225.1 %all-to-all-done.5 = bf16[320,4,4096]{2,0,1:T(8,128)(2,1)} async-done(((bf16[320,4,4096]{2,0,1:T(8,128)(2,1)}), bf16[320,4,4096]{2,0,1:T(8,128)(2,1)}, u32[]{:S(2)}, u32[]{:S(2)}) %all-to-all-start.5) | async-done | bytes 10485792 | tf_op jit(solution)/shard_map/all_to_all | solution.py:210
  2044.4 52.3 %concatenate.72 = bf16[1290,4096]{1,0:T(8,128)(2,1)} concatenate(bf16[5,4096]{1,0:T(8,128)(2,1)S(1)} %collective-permute-done, bf16[1280,4096]{1,0:T(8,128)(2,1)} %bitcast.58, bf16[5,4096]{1,0:T(8,128)(2,1)S(1)} %collective-permute-done.1), dimensions={0} | concatenate | bytes 21135360 | tf_op jit(solution)/shard_map/concatenate | solution.py:20
  2113.6 20.9 concatenate.73
  2146.4 47.3 %fusion.17 = (f32[1,1288,4104]{2,1,0:T(8,128)}, f32[1,1288,4104]{2,1,0:T(8,128)}) fusion(pred[4104]{0:T(1024)(128)(4,1)S(1)} %fusion.185, pred[1288]{0:T(1024)(128)(4,1)S(1)} %fusion.214, f32[1290,4106]{1,0:T(8,128)} %convert_element_type.185), kind=kLoop, calls=%fused_computation.44 | loop fusion | flops 47573568 | bytes 126868240 | tf_op jit(solution)/shard_map/stack | solution.py:226
  2193.7 141.6 %fusion.2 = f32[2,1280,4104]{2,1,0:T(8,128)} fusion(f32[1,1288,4104]{2,1,0:T(8,128)} %get-tuple-element.62, f32[1,1288,4104]{2,1,0:T(8,128)} %get-tuple-element.61), kind=kLoop, calls=%fused_computation.18 | loop fusion | flops 178606080 | bytes 84312576 | tf_op jit(solution)/shard_map/add | solution.py:168
  2335.3 181.9 %slice_add_fusion = f32[2,1280,4096]{2,1,0:T(8,128)} fusion(f32[2,1280,4104]{2,1,0:T(8,128)} %fusion.2), kind=kLoop, calls=%fused_computation.33 | loop fusion | flops 83886080 | bytes 419430400 | tf_op jit(solution)/shard_map/add | solution.py:168
  2517.2 22.4 fusion.23
  (126 shorter events, 321.1 us)
Async XLA Ops:
  10.7 230.4 %all-to-all-start = ((bf16[4,320,4096]{2,1,0:T(8,128)(2,1)}), bf16[4,320,4096]{2,1,0:T(8,128)(2,1)}, u32[]{:S(2)}, u32[]{:S(2)}) async-start(bf16[4,320,4096]{2,1,0:T(8,128)(2,1)} %bitcast.193), calls=%async_computation | async-start | bytes 20971520 | tf_op jit(solution)/shard_map/all_to_all | solution.py:185
  17.5 373.1 %copy-start.4 = (f32[128,128]{1,0:T(8,128)}, f32[128,128]{1,0:T(8,128)S(1)}, u32[]{:S(2)}) copy-start(f32[128,128]{1,0:T(8,128)S(1)} %get-tuple-element.75) | copy-start | bytes 196612
  17.5 373.1 %copy-start.6 = (f32[128,128]{1,0:T(8,128)}, f32[128,128]{1,0:T(8,128)S(1)}, u32[]{:S(2)}) copy-start(f32[128,128]{1,0:T(8,128)S(1)} %get-tuple-element.76) | copy-start | bytes 196612
  284.8 18.9 copy-start
  380.2 123.7 %all-to-all-start.1 = ((bf16[320,32,256]{2,0,1:T(8,128)(2,1)}), bf16[320,32,256]{2,0,1:T(8,128)(2,1)}, u32[]{:S(2)}, u32[]{:S(2)}) async-start(bf16[320,32,256]{2,0,1:T(8,128)(2,1)} %copy.258), calls=%async_computation.1 | async-start | bytes 10485760 | tf_op jit(solution)/shard_map/all_to_all | solution.py:198
  448.4 62.1 %copy-start.8 = (s32[2,8193]{1,0:T(2,128)S(1)}, s32[2,8193]{1,0:T(2,128)}, u32[]{:S(2)}) copy-start(s32[2,8193]{1,0:T(2,128)} %param.13) | copy-start | bytes 196636
  503.9 121.3 %all-to-all-start.2 = ((bf16[320,32,256]{2,0,1:T(8,128)(2,1)}), bf16[320,32,256]{2,0,1:T(8,128)(2,1)}, u32[]{:S(2)}, u32[]{:S(2)}) async-start(bf16[320,32,256]{2,0,1:T(8,128)(2,1)} %copy.263), calls=%async_computation.2 | async-start | bytes 10485760 | tf_op jit(solution)/shard_map/all_to_all | solution.py:199
  656.7 22.9 slice-start
  656.7 22.9 slice-start.1
  656.7 22.9 slice-start.2
  839.0 17.9 copy-start.2
  884.7 18.2 copy-start.3
  884.7 33.8 %slice-start.3 = ((s8[10485760]{0:T(1024)(128)(4,1)}), s8[4194304]{0:T(1024)(128)(4,1)S(1)}, s32[]{:S(2)}) async-start(s8[10485760]{0:T(1024)(128)(4,1)} %bitcast.194), calls=%async_computation.9 | async-start | bytes 8388608
  884.7 33.8 %slice-start.4 = ((s8[10485760]{0:T(1024)(128)(4,1)}), s8[4194304]{0:T(1024)(128)(4,1)S(1)}, s32[]{:S(2)}) async-start(s8[10485760]{0:T(1024)(128)(4,1)} %bitcast.194), calls=%async_computation.10 | async-start | bytes 8388608
  902.9 15.6 slice-start.5
  957.8 7.8 copy-start.1
  983.4 120.9 %all-to-all-start.3 = ((bf16[32,320,256]{2,1,0:T(8,128)(2,1)}), bf16[32,320,256]{2,1,0:T(8,128)(2,1)}, u32[]{:S(2)}, u32[]{:S(2)}) async-start(bf16[32,320,256]{2,1,0:T(8,128)(2,1)} %copy.292), calls=%async_computation.3 | async-start | bytes 10485760 | tf_op jit(solution)/shard_map/all_to_all | solution.py:205
  1104.3 120.9 %all-to-all-start.4 = ((bf16[32,320,256]{2,1,0:T(8,128)(2,1)}), bf16[32,320,256]{2,1,0:T(8,128)(2,1)}, u32[]{:S(2)}, u32[]{:S(2)}) async-start(bf16[32,320,256]{2,1,0:T(8,128)(2,1)} %copy.295), calls=%async_computation.4 | async-start | bytes 10485760 | tf_op jit(solution)/shard_map/all_to_all | solution.py:206
  1680.4 17.7 copy-start.5
  1680.4 17.8 copy-start.7
  1802.8 231.8 %all-to-all-start.5 = ((bf16[320,4,4096]{2,0,1:T(8,128)(2,1)}), bf16[320,4,4096]{2,0,1:T(8,128)(2,1)}, u32[]{:S(2)}, u32[]{:S(2)}) async-start(bf16[320,4,4096]{2,0,1:T(8,128)(2,1)} %copy.306), calls=%async_computation.5 | async-start | bytes 20971520 | tf_op jit(solution)/shard_map/all_to_all | solution.py:210
  2035.4 4.4 collective-permute-start
  2037.9 6.5 collective-permute-start.1
  2097.9 11.5 collective-permute-start.2
  2102.3 11.3 collective-permute-start.3
where the time goes:
time: 2590 us; the launch traced here: 2540 us
  waiting for transfers between devices  773 us (30%)
  local copies, waits for them, and re-layouts  686 us (26%)
  other arithmetic  531 us (21%)
  matrix products  501 us (19%)
  starting transfers between devices  48.7 us (2%)
    dot_general x29, matrix products, contract(): jnp.einsum(pattern, left_arg, right_arg, precision=lax.Precision.HIGH, pr...  501 us
    add x2, other arithmetic, box_sum(): running + lax.slice_in_dim(values, offset, offset + length, axis=dim_index)  323 us
    all_to_all x1, waiting for transfers between devices, per_device(): lax.all_to_all(filtered_rows, 'tm', split_axis=1, concat_axis=0, tiled=True)  225 us
    all_to_all x1, waiting for transfers between devices, per_device(): lax.all_to_all(tiles, 'tm', split_axis=0, concat_axis=1, tiled=True)  224 us
    rev x1, local copies, waits for them, and re-layouts, unfold_half(): rest_im = -jnp.flip(jnp.flip(lower_im[:, 1:, :], 1), 2)  159 us
    rev x1, local copies, waits for them, and re-layouts, unfold_half(): rest_re = jnp.flip(jnp.flip(lower_re[:, 1:, :], 1), 2)  159 us
    all_to_all x1, waiting for transfers between devices, per_device(): lax.all_to_all(filt_im, ('chan', 'tm'), split_axis=0, concat_axis=1, tile...  89.1 us
    all_to_all x1, waiting for transfers between devices, per_device(): lax.all_to_all(spec_im, ('chan', 'tm'), split_axis=1, concat_axis=0, tile...  89.1 us
  transfers between devices with their start and end apart: 10, of which 9 were waited for; matrix products, arithmetic and copies ran while one was open for 6% of the time, Pallas kernels for 0%

commit v1 on v0

v1 whole, which is shorter than its diff:
```python
import math

import jax
import jax.numpy as jnp
from jax import lax
from jax.experimental import pallas as pl
from jax.experimental.pallas import tpu as pltpu
from jax.sharding import PartitionSpec as P

NC = 10240
NT = 16384
TF = 128
R = 4


def contract(pattern, left_arg, right_arg):
    return jnp.einsum(
        pattern,
        left_arg,
        right_arg,
        precision=lax.Precision.HIGH,
        preferred_element_type=jnp.float32,
    )


def rotations(row_digits, col_digits, length):
    phase_int = row_digits[:, None] * col_digits[None, :] % length
    angles = phase_int.astype(jnp.float32) * (2.0 * math.pi / length)
    return (jnp.cos(angles), jnp.sin(angles))


def split_hi_lo(values):
    high = values.astype(jnp.bfloat16)
    low = (values - high.astype(jnp.float32)).astype(jnp.bfloat16)
    return high, low


def dot(left, right):
    return jnp.dot(left, right, preferred_element_type=jnp.float32)


def forward_kernel(x_ref, w_ref, tc_ref, ts_ref, b_ref, o_ref, held):
    rows = held.shape[0]
    half = TF // 2

    def one(row, carry):
        x = x_ref[:, pl.ds(row, 1)].reshape(TF, TF)
        first = dot(w_ref[...], jnp.concatenate([x, x], axis=0))
        first_re, first_im = first[:TF], first[TF:]
        tw_cos, tw_sin = tc_ref[...], ts_ref[...]
        turned_re = first_re * tw_cos + first_im * tw_sin
        turned_im = first_im * tw_cos - first_re * tw_sin
        high, low = split_hi_lo(jnp.concatenate([turned_re, turned_im], axis=1))
        wide = dot(high, b_ref[...])
        spec = wide[:, :TF] + wide[:, TF:] + dot(low, b_ref[:, :TF])
        lane = lax.broadcasted_iota(jnp.int32, (8, TF), 1)
        line = lax.broadcasted_iota(jnp.int32, (8, TF), 0)
        signs = jnp.where(lane % 2 == 0, 1.0, -1.0)
        highest = jnp.sum(turned_re[:8] * signs, axis=1, keepdims=True)
        top = jnp.where((lane == half) & (line == 0), highest, spec[:8])
        held[pl.ds(row, 1)] = jnp.concatenate([top, spec[8:]], axis=0)[None]
        return carry

    lax.fori_loop(0, rows, one, 0, unroll=4)
    o_ref[...] = jnp.swapaxes(held[...], 0, 1).astype(jnp.bfloat16)


def time_forward(series):
    blocks, row_count, depth, _ = series.shape
    rows = 16
    half = TF // 2
    digits = jnp.arange(TF, dtype=jnp.int32)
    cos_w, sin_w = rotations(digits, digits, TF)
    tw_cos, tw_sin = rotations(digits, digits, TF * TF)
    w_high, w_low = split_hi_lo(jnp.concatenate([cos_w, -sin_w], axis=0))
    w = jnp.concatenate([w_high, w_low], axis=1)
    cos_k, sin_k = cos_w[:, :half], sin_w[:, :half]
    b = jnp.concatenate(
        [
            jnp.concatenate([cos_k, -sin_k], axis=1),
            jnp.concatenate([sin_k, cos_k], axis=1),
        ],
        axis=0,
    )
    b = jnp.concatenate(split_hi_lo(b), axis=1)
    whole = lambda i: (0, 0)
    return pl.pallas_call(
        forward_kernel,
        grid=(row_count // rows,),
        in_specs=[
            pl.BlockSpec((blocks, rows, depth, TF), lambda i: (0, i, 0, 0)),
            pl.BlockSpec(w.shape, whole),
            pl.BlockSpec((TF, TF), whole),
            pl.BlockSpec((TF, TF), whole),
            pl.BlockSpec(b.shape, whole),
        ],
        out_specs=pl.BlockSpec((TF, rows, TF), lambda i: (0, i, 0)),
        out_shape=jax.ShapeDtypeStruct((TF, row_count, TF), jnp.bfloat16),
        scratch_shapes=[pltpu.VMEM((rows, TF, TF), jnp.float32)],
        compiler_params=pltpu.CompilerParams(vmem_limit_bytes=48 * 2**20),
        name="time_forward",
    )(series, w, tw_cos, tw_sin, b)


def inverse_kernel(p_ref, b_ref, tc_ref, ts_ref, w_ref, o_ref, held):
    rows = held.shape[0]
    blocks, _, depth, _ = o_ref.shape
    half = TF // 2
    held[...] = jnp.swapaxes(p_ref[...].astype(jnp.float32), 0, 1)

    def one(row, carry):
        part = held[pl.ds(row, 1)].reshape(TF, TF)
        packed = part.astype(jnp.bfloat16)
        mixed = dot(jnp.concatenate([packed, packed], axis=1), b_ref[...])
        mixed_re, mixed_im = mixed[:, :TF], mixed[:, TF:]
        lane = lax.broadcasted_iota(jnp.int32, (8, TF), 1)
        line = lax.broadcasted_iota(jnp.int32, (8, TF), 0)
        signs = jnp.where(lane % 2 == 0, 0.5, -0.5)
        fix = signs * part[:8, half : half + 1] - 0.5 * part[:8, 0:1]
        top = mixed_re[:8] + jnp.where(line == 0, fix, 0.0)
        mixed_re = jnp.concatenate([top, mixed_re[8:]], axis=0)
        tw_cos, tw_sin = tc_ref[...], ts_ref[...]
        turned_re = mixed_re * tw_cos - mixed_im * tw_sin
        turned_im = mixed_im * tw_cos + mixed_re * tw_sin
        high, low = split_hi_lo(jnp.concatenate([turned_re, turned_im], axis=0))
        tall = dot(w_ref[...], high)
        out = tall[:TF] + tall[TF:] + dot(w_ref[:TF, :], low)
        o_ref[:, pl.ds(row, 1)] = out.reshape(blocks, 1, depth, TF).astype(jnp.bfloat16)
        return carry

    lax.fori_loop(0, rows, one, 0, unroll=4)


def time_inverse(spec, blocks):
    row_count = spec.shape[1]
    rows = 16
    half = TF // 2
    depth = TF // blocks
    digits = jnp.arange(TF, dtype=jnp.int32)
    cos_w, sin_w = rotations(digits, digits, TF)
    tw_cos, tw_sin = rotations(digits, digits, TF * TF)
    scale = 2.0 / (TF * TF)
    cos_j, sin_j = cos_w[:half], sin_w[:half]
    b = jnp.concatenate(
        [
            jnp.concatenate([cos_j, sin_j], axis=1),
            jnp.concatenate([-sin_j, cos_j], axis=1),
        ],
        axis=0,
    )
    b = jnp.concatenate(split_hi_lo(b), axis=0)
    w = jnp.concatenate(split_hi_lo(jnp.concatenate([cos_w, -sin_w], axis=1)), axis=0)
    whole = lambda i: (0, 0)
    return pl.pallas_call(
        inverse_kernel,
        grid=(row_count // rows,),
        in_specs=[
            pl.BlockSpec((TF, rows, TF), lambda i: (0, i, 0)),
            pl.BlockSpec(b.shape, whole),
            pl.BlockSpec((TF, TF), whole),
            pl.BlockSpec((TF, TF), whole),
            pl.BlockSpec(w.shape, whole),
        ],
        out_specs=pl.BlockSpec((blocks, rows, depth, TF), lambda i: (0, i, 0, 0)),
        out_shape=jax.ShapeDtypeStruct((blocks, row_count, depth, TF), jnp.bfloat16),
        scratch_shapes=[pltpu.VMEM((rows, TF, TF), jnp.float32)],
        compiler_params=pltpu.CompilerParams(vmem_limit_bytes=48 * 2**20),
        name="time_inverse",
    )(spec, b, tw_cos * scale, tw_sin * scale, w)


def reversed_waves(values):
    along_outer = jnp.roll(jnp.flip(values, 0), 1, axis=0)
    along_inner = jnp.flip(along_outer, 1)
    first_row = jnp.roll(along_inner[0:1], 1, axis=1)
    return jnp.concatenate([first_row, along_inner[1:]], axis=0)


def channel_filter(
    pencil_re, pencil_im, position, lower_bound, upper_bound, top_low, top_high, packed
):
    devices = position.shape[0]
    row_depth = NC // devices
    columns = pencil_re.shape[1]
    part_re = pencil_re.astype(jnp.float32).reshape(devices, row_depth, columns)
    part_im = pencil_im.astype(jnp.float32).reshape(devices, row_depth, columns)
    outer_digits = jnp.arange(devices, dtype=jnp.int32)
    inner_digits = jnp.arange(row_depth, dtype=jnp.int32)
    cos_a, sin_a = rotations(outer_digits, position, devices)
    cos_b, sin_b = rotations(inner_digits, inner_digits, row_depth)
    tw_cos, tw_sin = rotations(outer_digits, inner_digits, NC)
    tw_cos = tw_cos[:, :, None]
    tw_sin = tw_sin[:, :, None]
    first_re = contract("pbf,kp->kbf", part_re, cos_a) + contract("pbf,kp->kbf", part_im, sin_a)
    first_im = contract("pbf,kp->kbf", part_im, cos_a) - contract("pbf,kp->kbf", part_re, sin_a)
    turned_re = first_re * tw_cos + first_im * tw_sin
    turned_im = first_im * tw_cos - first_re * tw_sin
    wave_re = contract("kbf,jb->kjf", turned_re, cos_b) + contract("kbf,jb->kjf", turned_im, sin_b)
    wave_im = contract("kbf,jb->kjf", turned_im, cos_b) - contract("kbf,jb->kjf", turned_re, sin_b)
    number = outer_digits[:, None] + devices * inner_digits[None, :]
    folded = jnp.minimum(number, NC - number)
    passing = (
        (folded[:, :, None] >= lower_bound[None, None, :])
        & (folded[:, :, None] <= upper_bound[None, None, :])
    ).astype(jnp.float32)
    top_pass = ((folded >= top_low) & (folded <= top_high)).astype(jnp.float32)
    first_pass = passing[:, :, 0]
    column_re = wave_re[:, :, 0]
    column_im = wave_im[:, :, 0]
    mirror_re = reversed_waves(column_re)
    mirror_im = reversed_waves(column_im)
    even_part = (first_pass + top_pass) * 0.5
    odd_part = (first_pass - top_pass) * 0.5
    split_re = even_part * column_re + odd_part * mirror_re
    split_im = even_part * column_im - odd_part * mirror_im
    wave_re = wave_re * passing
    wave_im = wave_im * passing
    wave_re = wave_re.at[:, :, 0].set(packed * split_re + (1.0 - packed) * wave_re[:, :, 0])
    wave_im = wave_im.at[:, :, 0].set(packed * split_im + (1.0 - packed) * wave_im[:, :, 0])
    back_re = contract("kjf,jb->kbf", wave_re, cos_b) - contract("kjf,jb->kbf", wave_im, sin_b)
    back_im = contract("kjf,jb->kbf", wave_im, cos_b) + contract("kjf,jb->kbf", wave_re, sin_b)
    untwist_re = back_re * tw_cos - back_im * tw_sin
    untwist_im = back_im * tw_cos + back_re * tw_sin
    out_re = contract("kbf,kp->pbf", untwist_re, cos_a) - contract("kbf,kp->pbf", untwist_im, sin_a)
    out_im = contract("kbf,kp->pbf", untwist_im, cos_a) + contract("kbf,kp->pbf", untwist_re, sin_a)
    return (
        (out_re / NC).reshape(NC, columns).astype(jnp.bfloat16),
        (out_im / NC).reshape(NC, columns).astype(jnp.bfloat16),
    )


EDGE = 16
SIDE = 128


def tensor_kernel(
    where_ref, above_ref, mid_ref, below_ref, head_ref, foot_ref, left_ref, right_ref, o_ref
):
    step = pl.program_id(0)
    steps = pl.num_programs(0)
    rows, width = mid_ref.shape
    tall = rows + 2 * EDGE
    chunk = 512
    for start in range(0, width, chunk):
        low, high = start - SIDE, start + chunk + SIDE
        inner = slice(max(low, 0), min(high, width))
        above = jnp.where(step == 0, head_ref[:, inner], above_ref[:, inner])
        below = jnp.where(step == steps - 1, foot_ref[:, inner], below_ref[:, inner])
        cells = jnp.concatenate([above, mid_ref[:, inner], below], axis=0).astype(jnp.float32)
        pieces = [cells]
        lines = pl.ds(pl.multiple_of(step * rows, 16), tall)
        if low < 0:
            pieces = [left_ref[lines, :].astype(jnp.float32)] + pieces
        if high > width:
            pieces = pieces + [right_ref[lines, :].astype(jnp.float32)]
        cells = jnp.concatenate(pieces, axis=1) if len(pieces) > 1 else cells
        wide = cells.shape[1]
        row_at = where_ref[0] + step * rows - EDGE + lax.broadcasted_iota(jnp.int32, (tall, 1), 0)
        col_at = where_ref[1] + low + lax.broadcasted_iota(jnp.int32, (1, wide), 1)
        inside = ((row_at >= 0) & (row_at < NC)) & ((col_at >= 0) & (col_at < NT))
        grad_chan = pltpu.roll(cells, tall - 1, 0) - pltpu.roll(cells, 1, 0)
        grad_time = pltpu.roll(cells, wide - 1, 1) - pltpu.roll(cells, 1, 1)
        grad_time = jnp.where(inside, grad_time, 0.0)

        def box(values, axis):
            length = values.shape[axis]
            two = values + pltpu.roll(values, 1, axis)
            four = two + pltpu.roll(two, 2, axis)
            eight = four + pltpu.roll(four, length - R, axis)
            return eight + pltpu.roll(values, R, axis)

        def smooth(values):
            return box(box(values, 0)[EDGE : EDGE + rows], 1)[:, SIDE : SIDE + chunk]

        cross = smooth(grad_chan * grad_time)
        along = smooth(grad_time * grad_time)
        area = (2 * R + 1) * (2 * R + 1)
        o_ref[:, start : start + chunk] = -cross / (along + 4e-5 * area)


def from_before(values, axis):
    count = lax.axis_size(axis)
    return lax.ppermute(values, axis, [(i, i + 1) for i in range(count - 1)])


def from_after(values, axis):
    count = lax.axis_size(axis)
    return lax.ppermute(values, axis, [(i + 1, i) for i in range(count - 1)])


def tensor_slowness(cells):
    tile_chan, tile_time = cells.shape
    head = from_before(cells[tile_chan - EDGE :], "chan")
    foot = from_after(cells[:EDGE], "chan")

    def strip(cols):
        return jnp.concatenate([head[:, cols], cells[:, cols], foot[:, cols]], axis=0)

    left = from_before(strip(slice(tile_time - SIDE, tile_time)), "tm")
    right = from_after(strip(slice(0, SIDE)), "tm")
    where = jnp.stack(
        [lax.axis_index("chan") * tile_chan, lax.axis_index("tm") * tile_time]
    ).astype(jnp.int32)
    rows = 64
    ratio = rows // EDGE
    last = tile_chan // EDGE - 1
    whole = lambda i: (0, 0)
    return pl.pallas_call(
        tensor_kernel,
        grid=(tile_chan // rows,),
        in_specs=[
            pl.BlockSpec(memory_space=pltpu.SMEM),
            pl.BlockSpec((EDGE, tile_time), lambda i: (jnp.maximum(i * ratio - 1, 0), 0)),
            pl.BlockSpec((rows, tile_time), lambda i: (i, 0)),
            pl.BlockSpec((EDGE, tile_time), lambda i: (jnp.minimum((i + 1) * ratio, last), 0)),
            pl.BlockSpec((EDGE, tile_time), whole),
            pl.BlockSpec((EDGE, tile_time), whole),
            pl.BlockSpec((tile_chan + 2 * EDGE, SIDE), whole),
            pl.BlockSpec((tile_chan + 2 * EDGE, SIDE), whole),
        ],
        out_specs=pl.BlockSpec((rows, tile_time), lambda i: (i, 0)),
        out_shape=jax.ShapeDtypeStruct((tile_chan, tile_time), jnp.float32),
        compiler_params=pltpu.CompilerParams(vmem_limit_bytes=48 * 2**20),
        name="tensor_slowness",
    )(where, cells, cells, cells, head, foot, left, right)


def per_device(record, channel_ok, fan_bounds):
    chan_count = lax.axis_size("chan")
    time_count = lax.axis_size("tm")
    devices = chan_count * time_count
    tile_chan, tile_time = record.shape
    row_count = tile_chan // time_count
    half = TF // 2
    digits = TF // devices
    tiles = record * channel_ok.astype(jnp.bfloat16)[:, None]
    tiles = tiles.reshape(time_count, row_count, tile_time // TF, TF)
    series = lax.all_to_all(tiles, "tm", split_axis=0, concat_axis=0)
    block_index = lax.axis_index("chan") * time_count + lax.axis_index("tm")
    top_low = fan_bounds[0, NT // 2]
    top_high = fan_bounds[1, NT // 2]
    columns = digits * half
    ordered = (
        fan_bounds[:, : NT // 2].reshape(2, TF // 2, TF).transpose(0, 2, 1).reshape(2, NT // 2)
    )
    packed = (block_index == 0).astype(jnp.float32)
    window = lax.dynamic_slice_in_dim(ordered, block_index * columns, columns, 1)
    slot_index = jnp.arange(devices, dtype=jnp.int32)
    spec = time_forward(series).reshape(devices, digits, row_count, TF)
    pencil = lax.all_to_all(spec, ("chan", "tm"), split_axis=0, concat_axis=0)

    def flat(part):
        return part.transpose(0, 2, 1, 3).reshape(NC, columns)

    def folded(part):
        return part.reshape(devices, row_count, digits, half).transpose(0, 2, 1, 3)

    filt_re, filt_im = channel_filter(
        flat(pencil[..., :half]),
        flat(pencil[..., half:]),
        slot_index,
        window[0],
        window[1],
        top_low,
        top_high,
        packed,
    )
    filt = jnp.concatenate([folded(filt_re), folded(filt_im)], axis=3)
    back = lax.all_to_all(filt, ("chan", "tm"), split_axis=0, concat_axis=0)
    rows = time_inverse(back.reshape(TF, row_count, TF), time_count)
    rows = lax.all_to_all(rows, "tm", split_axis=0, concat_axis=0)
    return tensor_slowness(rows.reshape(tile_chan, tile_time))


def solution(mesh):
    in_specs = (P("chan", "tm"), P("chan"), P())
    out_specs = P("chan", "tm")
    return jax.shard_map(
        per_device, mesh=mesh, in_specs=in_specs, out_specs=out_specs, check_vma=False
    )
```

time: 2590 us -> 1800 us (0.69); the launches traced: 2540 us -> 1780 us
  local copies, waits for them, and re-layouts: 686 us -> 205 us
  other arithmetic: 531 us -> 103 us
  Pallas kernels: 0 us -> 285 us
  matrix products: 501 us -> 241 us
  blocking collectives: 0 us -> 233 us
  waiting for transfers between devices: 773 us -> 681 us
    add x4 -> x0, other arithmetic: 343 us -> none  [the longest x2 323 us: box_sum(): running + lax.slice_in_dim(values, offset, offset + length, axis=dim_index)]
    rev x4 -> x0, local copies, waits for them, and re-layouts: 318 us -> none  [the longest x1 159 us: unfold_half(): rest_im = -jnp.flip(jnp.flip(lower_im[:, 1:, :], 1), 2)]
    pallas_call x0 -> x3, Pallas kernels: none -> 285 us  [the longest x1 144 us: tensor_slowness(): pl.pallas_call(tensor_kernel, grid=(tile_chan // rows,), in_specs=[pl.Blo...]
    dot_general x29 -> x16, matrix products: 501 us -> 241 us  [contract(): jnp.einsum(pattern, left_arg, right_arg, precision=lax.Precision.HIGH, pr...]
    all_to_all x0 -> x1, blocking collectives: none -> 233 us  [per_device(): rows = lax.all_to_all(rows, 'tm', split_axis=0, concat_axis=0)]
    all_to_all x6 -> x3, waiting for transfers between devices: 759 us -> 673 us  [the longest x1 228 us: per_device(): back = lax.all_to_all(filt, ('chan', 'tm'), split_axis=0, concat_axis=0)]
    convert_element_type x6 -> x0, local copies, waits for them, and re-layouts: 64.6 us -> none  [the longest x2 29.1 us: time_inverse(): return (result / NT).reshape(row_count, NT).astype(jnp.bfloat16)]
    concatenate x2 -> x1, local copies, waits for them, and re-layouts: 73.2 us -> 15.1 us  [per_device(): filt = jnp.concatenate([folded(filt_re), folded(filt_im)], axis=3)]
  transfers between devices with their start and end apart: 10 -> 7, of which waited for: 9 -> 6; matrix products, arithmetic and copies ran while one was open for 6% -> 0% of each run, Pallas kernels for 0% -> 0%
where the time goes in v1:
time: 1800 us; the launch traced here: 1780 us
  waiting for transfers between devices  681 us (38%)
  Pallas kernels  285 us (16%)
  matrix products  241 us (13%)
  blocking collectives  233 us (13%)
  local copies, waits for them, and re-layouts  205 us (11%)
  other arithmetic  103 us (6%)
  starting transfers between devices  35 us (2%)
    dot_general x16, matrix products, contract(): jnp.einsum(pattern, left_arg, right_arg, precision=lax.Precision.HIGH, pr...  241 us
    all_to_all x1, blocking collectives, per_device(): rows = lax.all_to_all(rows, 'tm', split_axis=0, concat_axis=0)  233 us
    all_to_all x1, waiting for transfers between devices, per_device(): back = lax.all_to_all(filt, ('chan', 'tm'), split_axis=0, concat_axis=0)  228 us
    all_to_all x1, waiting for transfers between devices, per_device(): series = lax.all_to_all(tiles, 'tm', split_axis=0, concat_axis=0)  223 us
    all_to_all x1, waiting for transfers between devices, per_device(): pencil = lax.all_to_all(spec, ('chan', 'tm'), split_axis=0, concat_axis=0)  222 us
    pallas_call x1, Pallas kernels, tensor_slowness(): pl.pallas_call(tensor_kernel, grid=(tile_chan // rows,), in_specs=[pl.Blo...  144 us
    pallas_call x1, Pallas kernels, time_inverse(): pl.pallas_call(inverse_kernel, grid=(row_count // rows,), in_specs=[pl.Bl...  89.7 us
    pallas_call x1, Pallas kernels, time_forward(): pl.pallas_call(forward_kernel, grid=(row_count // rows,), in_specs=[pl.Bl...  51.5 us
  transfers between devices with their start and end apart: 7, of which 6 were waited for; matrix products, arithmetic and copies ran while one was open for 0% of the time, Pallas kernels for 0%

profile of v1, /device:TPU:19, one launch (start us, length us, event | category | flops | bytes accessed | tf_op | source)
XLA Modules:
  0.0 1783.2 jit_solution(15967780574721894481)
XLA Ops:
  0.7 10.0 multiply_bitcast_fusion
  10.7 11.4 copy.246
  22.1 6.0 all-to-all-start
  29.3 223.1 %all-to-all-done.x_ref = bf16[4,320,32,128]{3,2,1,0:T(8,128)(2,1)} async-done(((bf16[4,320,32,128]{3,2,1,0:T(8,128)(2,1)}), bf16[4,320,32,128]{3,2,1,0:T(8,128)(2,1)}, u32[]{:S(2)}, u32[]{:S(2)}) %all-to-all-start) | async-done | bytes 10485792 | tf_op jit(solution)/shard_map/all_to_all | solution.py:338
  252.5 51.5 %time_forward.1 = bf16[128,320,128]{2,1,0:T(8,128)(2,1)} custom-call(bf16[4,320,32,128]{3,2,1,0:T(8,128)(2,1)} %all-to-all-done.x_ref, bf16[256,256]{1,0:T(8,128)(2,1)S(1)} %pad_maximum_fusion.4.w_ref, f32[128,128]{1,0:T(8,128)S(1)} %get-tuple-element.62.tc_ref, f32[128,128]{1,0:T(8,128)S(1)} %get-tuple-element.61.ts_ref, ...), custom_call_target="tpu_custom_call" | custom-call | tf_op jit(solution)/shard_map/time_forward/pallas_call | solution.py:87
  304.0 8.4 all-to-all-start.1
  314.1 4.3 compare_and_fusion
  318.4 221.9 %all-to-all-done.1 = bf16[32,4,320,128]{3,2,1,0:T(8,128)(2,1)} async-done(((bf16[32,4,320,128]{3,2,1,0:T(8,128)(2,1)}), bf16[32,4,320,128]{3,2,1,0:T(8,128)(2,1)}, u32[]{:S(2)}, u32[]{:S(2)}) %all-to-all-start.1) | async-done | bytes 10485792 | tf_op jit(solution)/shard_map/all_to_all | solution.py:350
  540.3 18.7 %slice_bitcast_fusion.1 = (bf16[32,320,4,64]{3,1,2,0:T(8,128)(2,1)}, bf16[32,320,4,64]{3,1,2,0:T(8,128)(2,1)}) fusion(bf16[32,4,320,128]{3,2,1,0:T(8,128)(2,1)} %all-to-all-done.1), kind=kLoop, calls=%fused_computation.6 | loop fusion | bytes 20971520 | tf_op jit(solution)/shard_map/transpose | solution.py:353
  559.0 11.6 copy.192
  570.6 8.6 copy.194
  579.3 7.6 fusion.110
  586.9 5.6 fusion.116
  592.6 11.6 copy.195
  604.2 8.8 copy.197
  612.9 7.4 fusion.112
  620.4 18.3 %multiply_add_fusion = (f32[32,320,256]{2,0,1:T(8,128)S(1)}, f32[32,320,256]{2,0,1:T(8,128)}) fusion(f32[32,320]{0,1:T(8,128)S(1)} %copy.203, f32[32,320]{0,1:T(8,128)S(1)} %copy.198, f32[32,320,256]{2,0,1:T(8,128)} %fusion.110, f32[32,320,256]{2,0,1:T(8,128)} %fusion.116, f32[32,320,256]{2,0,1:T(8,128)} %fusion.112, bf16[32,320,256]{2,0,1:T(8,128)(2,1)} %copy.197), kind=kOutput, calls=%fused_computation.18 | convolution fusion | flops 524302336 | bytes 57753600 | tf_op jit(solution)/shard_map/pbf,kp->kbf/dot_general | solution.py:17
  638.7 23.1 %fusion.4 = f32[320,32,256]{2,0,1:T(8,128)} fusion(f32[32,320,256]{2,0,1:T(8,128)} %get-tuple-element.36), kind=kOutput, calls=%fused_computation.22 | convolution fusion | flops 5034086400 | bytes 20971520 | tf_op jit(solution)/shard_map/kbf,jb->kjf/dot_general | solution.py:17
  661.8 19.0 %fusion.2 = f32[320,32,256]{2,0,1:T(8,128)} fusion(f32[32,320,256]{2,0,1:T(8,128)S(1)} %bitcast.139), kind=kOutput, calls=%fused_computation.20 | convolution fusion | flops 5034086400 | bytes 20971520 | tf_op jit(solution)/shard_map/kbf,jb->kjf/dot_general | solution.py:17
  680.8 18.6 %fusion.8 = f32[320,32,256]{2,0,1:T(8,128)} fusion(f32[32,320,256]{2,0,1:T(8,128)S(1)} %get-tuple-element.35), kind=kOutput, calls=%fused_computation.26 | convolution fusion | flops 5034086400 | bytes 20971520 | tf_op jit(solution)/shard_map/kbf,jb->kjf/dot_general | solution.py:17
  699.4 18.6 %fusion.6 = f32[320,32,256]{2,0,1:T(8,128)} fusion(f32[32,320,256]{2,0,1:T(8,128)S(1)} %get-tuple-element.35), kind=kOutput, calls=%fused_computation.24 | convolution fusion | flops 5034086400 | bytes 20971520 | tf_op jit(solution)/shard_map/kbf,jb->kjf/dot_general | solution.py:17
  718.0 11.9 copy.208
  729.9 12.0 copy.209
  742.0 12.1 copy.216
  754.0 12.1 copy.217
  766.1 33.3 %broadcast_select_fusion.1 = (f32[32,320,256]{1,0,2:T(8,128)}, f32[32,320,256]{1,0,2:T(8,128)}, f32[32,320,256]{1,0,2:T(8,128)}, f32[32,320,256]{1,0,2:T(8,128)}) fusion(s32[256]{0:T(256)S(1)} %bitcast.161, s32[256]{0:T(256)S(1)} %bitcast.159, s32[32,320]{1,0:T(8,128)S(1)} %subtract_minimum_fusion.1, f32[320,32,256]{0,1,2:T(8,128)} %copy.208, ...), kind=kLoop, calls=%fused_computation.29 | loop fusion | flops 18350080 | bytes 83929088 | tf_op jit(solution)/shard_map/mul | solution.py:216
  809.5 12.0 copy.211
  821.5 17.8 fusion.22
  839.3 16.0 fusion.13
  855.3 11.9 copy.219
  867.2 17.9 %fusion.15 = f32[320,32,256]{2,0,1:T(8,128)} fusion(f32[32,320,256]{2,1,0:T(8,128)} %copy.219), kind=kOutput, calls=%fused_computation.36 | convolution fusion | flops 5034086400 | bytes 20971520 | tf_op jit(solution)/shard_map/kjf,jb->kbf/dot_general | solution.py:17
  885.1 15.7 fusion.20
  900.7 36.5 %fusion = (f32[32,320,256]{2,0,1:T(8,128)S(1)}, f32[32,320,256]{2,0,1:T(8,128)S(1)}) fusion(f32[32,320]{0,1:T(8,128)S(1)} %copy.203, f32[32,320]{0,1:T(8,128)S(1)} %copy.198, f32[320,32,256]{2,0,1:T(8,128)} %fusion.15, f32[320,32,256]{2,0,1:T(8,128)} %fusion.22, f32[320,32,256]{2,0,1:T(8,128)} %fusion.13, f32[320,32,256]{2,0,1:T(8,128)} %fusion.20), kind=kLoop, calls=%fused_computation.9 | loop fusion | flops 20971520 | bytes 62996480 | tf_op jit(solution)/shard_map/sub | solution.py:222
  937.2 8.1 fusion.118
  947.4 17.4 fusion.120
  964.8 14.7 multiply_convert_fusion
  979.5 8.6 copy.227
  988.2 14.7 multiply_convert_fusion.1
  1002.9 8.5 copy.226
  1011.4 11.8 pad_maximum_fusion
  1023.2 15.1 copy.228
  1038.3 8.0 all-to-all-start.2
  1046.8 227.6 %all-to-all-done.2 = bf16[32,4,320,128]{3,2,1,0:T(8,128)(2,1)} async-done(((bf16[32,4,320,128]{3,2,1,0:T(8,128)(2,1)}), bf16[32,4,320,128]{3,2,1,0:T(8,128)(2,1)}, u32[]{:S(2)}, u32[]{:S(2)}) %all-to-all-start.2) | async-done | bytes 10485792 | tf_op jit(solution)/shard_map/all_to_all | solution.py:369
  1274.4 89.7 %time_inverse.1 = bf16[4,320,32,128]{3,2,1,0:T(8,128)(2,1)} custom-call(bf16[128,320,128]{2,1,0:T(8,128)(2,1)} %bitcast.42.p_ref, bf16[256,256]{1,0:T(8,128)(2,1)S(1)} %pad_maximum_fusion.6.b_ref, f32[128,128]{1,0:T(8,128)S(1)} %get-tuple-element.64.tc_ref, f32[128,128]{1,0:T(8,128)S(1)} %get-tuple-element.63.ts_ref, ...), custom_call_target="tpu_custom_call" | custom-call | tf_op jit(solution)/shard_map/time_inverse/pallas_call | solution.py:154
  1364.1 232.9 %all_to_all.20 = bf16[4,320,32,128]{3,2,1,0:T(8,128)(2,1)} all-to-all(bf16[4,320,32,128]{3,2,1,0:T(8,128)(2,1)} %time_inverse.1), channel_id=1, replica_groups=mesh['chan'=8,'tm'=4] {'tm'}, dimensions={0} | all-to-all | bytes 20971520 | tf_op jit(solution)/shard_map/all_to_all | solution.py:371
  1597.0 18.6 %copy.278 = bf16[160,8,32,128]{3,1,2,0:T(8,128)(2,1)} copy(bf16[160,8,32,128]{3,2,1,0:T(8,128)(2,1)} %bitcast.147) | data formatting | bytes 20971520
  1616.6 4.1 collective-permute-start.1
  1639.0 143.8 %tensor_slowness.1 = f32[1280,4096]{1,0:T(8,128)} custom-call(s32[2]{0:T(128)S(1)} %pad_add_fusion.where_ref, bf16[1280,4096]{1,0:T(8,128)(2,1)} %bitcast.142, bf16[1280,4096]{1,0:T(8,128)(2,1)} %bitcast.143, bf16[1280,4096]{1,0:T(8,128)(2,1)} %bitcast.144, bf16[16,4096]{1,0:T(8,128)(2,1)S(1)} %collective-permute-done.head_ref, ...), custom_call_target="tpu_custom_call" | custom-call | tf_op jit(solution)/shard_map/tensor_slowness/pallas_call | solution.py:308
  (100 shorter events, 35.1 us)
Async XLA Ops:
  22.1 230.4 %all-to-all-start = ((bf16[4,320,32,128]{3,2,1,0:T(8,128)(2,1)}), bf16[4,320,32,128]{3,2,1,0:T(8,128)(2,1)}, u32[]{:S(2)}, u32[]{:S(2)}) async-start(bf16[4,320,32,128]{3,2,1,0:T(8,128)(2,1)} %bitcast.146), calls=%async_computation | async-start | bytes 20971520 | tf_op jit(solution)/shard_map/all_to_all | solution.py:338
  28.4 0.8 copy-start.5
  28.4 0.9 copy-start.7
  28.7 0.6 copy-start.9
  304.0 9.1 copy-start.11
  304.0 236.3 %all-to-all-start.1 = ((bf16[32,4,320,128]{3,2,1,0:T(8,128)(2,1)}), bf16[32,4,320,128]{3,2,1,0:T(8,128)(2,1)}, u32[]{:S(2)}, u32[]{:S(2)}) async-start(bf16[32,4,320,128]{3,2,1,0:T(8,128)(2,1)} %bitcast.145), calls=%async_computation.1 | async-start | bytes 20971520 | tf_op jit(solution)/shard_map/all_to_all | solution.py:350
  313.4 245.7 %copy-start.12 = (s32[320]{0:T(512)}, s32[320]{0:T(512)S(1)}, u32[]{:S(2)}) copy-start(s32[320]{0:T(512)S(1)} %iota_multiply_fusion.1) | copy-start | bytes 3844
  579.3 7.6 copy-start.4
  638.7 23.1 %slice-start = ((s8[10485760]{0:T(1024)(128)(4,1)}), s8[4194304]{0:T(1024)(128)(4,1)S(1)}, s32[]{:S(2)}) async-start(s8[10485760]{0:T(1024)(128)(4,1)} %bitcast.138), calls=%async_computation.4 | async-start | bytes 8388608
  638.7 23.1 %slice-start.1 = ((s8[10485760]{0:T(1024)(128)(4,1)}), s8[4194304]{0:T(1024)(128)(4,1)S(1)}, s32[]{:S(2)}) async-start(s8[10485760]{0:T(1024)(128)(4,1)} %bitcast.138), calls=%async_computation.5 | async-start | bytes 8388608
  638.7 23.1 %slice-start.2 = ((s8[10485760]{0:T(1024)(128)(4,1)}), s8[2097152]{0:T(1024)(128)(4,1)S(1)}, s32[]{:S(2)}) async-start(s8[10485760]{0:T(1024)(128)(4,1)} %bitcast.138), calls=%async_computation.6 | async-start | bytes 4194304
  766.1 40.5 %copy-start.13 = (s32[320]{0:T(512)S(1)}, s32[320]{0:T(512)}, u32[]{:S(2)}) copy-start(s32[320]{0:T(512)} %copy-done.12) | copy-start | bytes 3844
  821.5 17.8 copy-start.2
  867.2 17.9 %copy-start.3 = (f32[32,320,256]{2,1,0:T(8,128)S(1)}, f32[32,320,256]{2,1,0:T(8,128)}, u32[]{:S(2)}) copy-start(f32[32,320,256]{2,1,0:T(8,128)} %copy.219) | copy-start | bytes 31457284
  937.2 8.2 copy-start
  937.2 10.2 copy-start.1
  1038.3 8.0 copy-start.6
  1038.3 8.1 copy-start.10
  1038.3 8.1 copy-start.8
  1038.3 236.1 %all-to-all-start.2 = ((bf16[32,4,320,128]{3,2,1,0:T(8,128)(2,1)}), bf16[32,4,320,128]{3,2,1,0:T(8,128)(2,1)}, u32[]{:S(2)}, u32[]{:S(2)}) async-start(bf16[32,4,320,128]{3,2,1,0:T(8,128)(2,1)} %copy.228), calls=%async_computation.2 | async-start | bytes 20971520 | tf_op jit(solution)/shard_map/all_to_all | solution.py:369
  1616.6 8.1 collective-permute-start.1
  1621.9 4.8 collective-permute-start
  1626.7 9.7 collective-permute-start.2
  1630.0 9.0 collective-permute-start.3

commit v2 on v1

--- a/solution.py
+++ b/solution.py
@@ -1,3 +1,4 @@
+import functools
 import math
 
 import jax
@@ -13,16 +14,6 @@
 R = 4
 
 
-def contract(pattern, left_arg, right_arg):
-    return jnp.einsum(
-        pattern,
-        left_arg,
-        right_arg,
-        precision=lax.Precision.HIGH,
-        preferred_element_type=jnp.float32,
-    )
-
-
 def rotations(row_digits, col_digits, length):
     phase_int = row_digits[:, None] * col_digits[None, :] % length
     angles = phase_int.astype(jnp.float32) * (2.0 * math.pi / length)
@@ -37,6 +28,11 @@
 
 def dot(left, right):
     return jnp.dot(left, right, preferred_element_type=jnp.float32)
+
+
+def split_table(values):
+    high = lax.reduce_precision(values, 8, 7)
+    return high.astype(jnp.bfloat16), (values - high).astype(jnp.bfloat16)
 
 
 def forward_kernel(x_ref, w_ref, tc_ref, ts_ref, b_ref, o_ref, held):
@@ -72,7 +68,7 @@
     digits = jnp.arange(TF, dtype=jnp.int32)
     cos_w, sin_w = rotations(digits, digits, TF)
     tw_cos, tw_sin = rotations(digits, digits, TF * TF)
-    w_high, w_low = split_hi_lo(jnp.concatenate([cos_w, -sin_w], axis=0))
+    w_high, w_low = split_table(jnp.concatenate([cos_w, -sin_w], axis=0))
     w = jnp.concatenate([w_high, w_low], axis=1)
     cos_k, sin_k = cos_w[:, :half], sin_w[:, :half]
     b = jnp.concatenate(
@@ -82,7 +78,7 @@
         ],
         axis=0,
     )
-    b = jnp.concatenate(split_hi_lo(b), axis=1)
+    b = jnp.concatenate(split_table(b), axis=1)
     whole = lambda i: (0, 0)
     return pl.pallas_call(
         forward_kernel,
@@ -148,8 +144,8 @@
         ],
         axis=0,
     )
-    b = jnp.concatenate(split_hi_lo(b), axis=0)
-    w = jnp.concatenate(split_hi_lo(jnp.concatenate([cos_w, -sin_w], axis=1)), axis=0)
+    b = jnp.concatenate(split_table(b), axis=0)
+    w = jnp.concatenate(split_table(jnp.concatenate([cos_w, -sin_w], axis=1)), axis=0)
     whole = lambda i: (0, 0)
     return pl.pallas_call(
         inverse_kernel,
@@ -169,64 +165,148 @@
     )(spec, b, tw_cos * scale, tw_sin * scale, w)
 
 
-def reversed_waves(values):
-    along_outer = jnp.roll(jnp.flip(values, 0), 1, axis=0)
-    along_inner = jnp.flip(along_outer, 1)
-    first_row = jnp.roll(along_inner[0:1], 1, axis=1)
-    return jnp.concatenate([first_row, along_inner[1:]], axis=0)
-
-
-def channel_filter(
-    pencil_re, pencil_im, position, lower_bound, upper_bound, top_low, top_high, packed
-):
-    devices = position.shape[0]
-    row_depth = NC // devices
-    columns = pencil_re.shape[1]
-    part_re = pencil_re.astype(jnp.float32).reshape(devices, row_depth, columns)
-    part_im = pencil_im.astype(jnp.float32).reshape(devices, row_depth, columns)
-    outer_digits = jnp.arange(devices, dtype=jnp.int32)
-    inner_digits = jnp.arange(row_depth, dtype=jnp.int32)
-    cos_a, sin_a = rotations(outer_digits, position, devices)
-    cos_b, sin_b = rotations(inner_digits, inner_digits, row_depth)
-    tw_cos, tw_sin = rotations(outer_digits, inner_digits, NC)
-    tw_cos = tw_cos[:, :, None]
-    tw_sin = tw_sin[:, :, None]
-    first_re = contract("pbf,kp->kbf", part_re, cos_a) + contract("pbf,kp->kbf", part_im, sin_a)
-    first_im = contract("pbf,kp->kbf", part_im, cos_a) - contract("pbf,kp->kbf", part_re, sin_a)
-    turned_re = first_re * tw_cos + first_im * tw_sin
-    turned_im = first_im * tw_cos - first_re * tw_sin
-    wave_re = contract("kbf,jb->kjf", turned_re, cos_b) + contract("kbf,jb->kjf", turned_im, sin_b)
-    wave_im = contract("kbf,jb->kjf", turned_im, cos_b) - contract("kbf,jb->kjf", turned_re, sin_b)
-    number = outer_digits[:, None] + devices * inner_digits[None, :]
-    folded = jnp.minimum(number, NC - number)
-    passing = (
-        (folded[:, :, None] >= lower_bound[None, None, :])
-        & (folded[:, :, None] <= upper_bound[None, None, :])
-    ).astype(jnp.float32)
-    top_pass = ((folded >= top_low) & (folded <= top_high)).astype(jnp.float32)
-    first_pass = passing[:, :, 0]
-    column_re = wave_re[:, :, 0]
-    column_im = wave_im[:, :, 0]
-    mirror_re = reversed_waves(column_re)
-    mirror_im = reversed_waves(column_im)
-    even_part = (first_pass + top_pass) * 0.5
-    odd_part = (first_pass - top_pass) * 0.5
-    split_re = even_part * column_re + odd_part * mirror_re
-    split_im = even_part * column_im - odd_part * mirror_im
-    wave_re = wave_re * passing
-    wave_im = wave_im * passing
-    wave_re = wave_re.at[:, :, 0].set(packed * split_re + (1.0 - packed) * wave_re[:, :, 0])
-    wave_im = wave_im.at[:, :, 0].set(packed * split_im + (1.0 - packed) * wave_im[:, :, 0])
-    back_re = contract("kjf,jb->kbf", wave_re, cos_b) - contract("kjf,jb->kbf", wave_im, sin_b)
-    back_im = contract("kjf,jb->kbf", wave_im, cos_b) + contract("kjf,jb->kbf", wave_re, sin_b)
-    untwist_re = back_re * tw_cos - back_im * tw_sin
-    untwist_im = back_im * tw_cos + back_re * tw_sin
-    out_re = contract("kbf,kp->pbf", untwist_re, cos_a) - contract("kbf,kp->pbf", untwist_im, sin_a)
-    out_im = contract("kbf,kp->pbf", untwist_im, cos_a) + contract("kbf,kp->pbf", untwist_re, sin_a)
-    return (
-        (out_re / NC).reshape(NC, columns).astype(jnp.bfloat16),
-        (out_im / NC).reshape(NC, columns).astype(jnp.bfloat16),
-    )
+def quarter_turn(values):
+    width = values.shape[-1]
+    lane = lax.broadcasted_iota(jnp.int32, (1, width), 1)
+    return pltpu.roll(values, width // 2, 1) * jnp.where(lane < width // 2, 1.0, -1.0)
+
+
+def fast_fourier(parts, sign):
+    count = len(parts)
+    if count == 1:
+        return parts
+    even = fast_fourier(parts[0::2], sign)
+    odd = fast_fourier(parts[1::2], sign)
+    low, high = [], []
+    for k in range(count // 2):
+        if k == 0:
+            turned = odd[k]
+        elif 4 * k == count:
+            turned = quarter_turn(odd[k]) * sign
+        else:
+            angle = 2.0 * math.pi * k / count
+            turned = odd[k] * math.cos(angle) + quarter_turn(odd[k]) * (sign * math.sin(angle))
+        low.append(even[k] + turned)
+        high.append(even[k] - turned)
+    return low + high
+
+
+def channel_kernel(sizes, flag_ref, bound_ref, tc_ref, ts_ref, f_ref, g_ref, *refs):
+    x_refs, o_refs, held = refs[: len(sizes)], refs[len(sizes) : -1], refs[-1]
+    count, depth, width = held.shape
+    step = pl.program_id(0)
+    first = flag_ref[0] == 1
+    half = width // 2
+    lane = lax.broadcasted_iota(jnp.int32, (1, width), 1)
+    lines = 16
+
+    def transform(matrix_ref, values):
+        high, low = split_hi_lo(jnp.concatenate([values, quarter_turn(values)], axis=0))
+        wide = dot(matrix_ref[:depth], jnp.concatenate([high, low], axis=1))
+        return wide[:, :width] + wide[:, width:] + dot(matrix_ref[depth:], high)
+
+    @pl.when((step > 0) | first)
+    def _():
+        drop = jnp.where((step == 1) & first, 1.0, 0.0)
+        kept = jnp.where(
+            step == 0,
+            (lane == 0).astype(jnp.float32),
+            1.0 - drop * (lane == half).astype(jnp.float32),
+        )
+
+        def gather(x_ref, offset, index, carry):
+            here = pl.ds(pl.multiple_of(index * lines, lines), lines)
+            there = pl.ds(pl.multiple_of(offset + index * lines, lines), lines)
+            parts = []
+            for p in range(count):
+                part = x_ref[p, 0, here, :].astype(jnp.float32)
+                parts.append(jnp.where(step == 0, pltpu.roll(part, half, 1), part) * kept)
+            for p, part in enumerate(fast_fourier(parts, 1.0)):
+                held[p, there, :] = part
+            return carry
+
+        offset = 0
+        for x_ref, size in zip(x_refs, sizes):
+            lax.fori_loop(0, size // lines, functools.partial(gather, x_ref, offset), 0)
+            offset += size
+        lower, upper = bound_ref[0, 0:1, :], bound_ref[0, 1:2, :]
+
+        def middle(outer, carry):
+            turn_cos, turn_sin = tc_ref[outer], ts_ref[outer]
+            values = held[outer]
+            values = values * turn_cos + pltpu.roll(values, half, 1) * turn_sin
+            wave = transform(f_ref, values)
+            number = outer + count * lax.broadcasted_iota(jnp.int32, (depth, width), 0)
+            folded = jnp.minimum(number, count * depth - number)
+            wave = jnp.where((folded >= lower) & (folded <= upper), wave, 0.0)
+            back = transform(g_ref, wave)
+            held[outer] = back * turn_cos - pltpu.roll(back, half, 1) * turn_sin
+            return carry
+
+        lax.fori_loop(0, count, middle, 0)
+        placed = lane == jnp.where((step == 1) & first, half, -1)
+
+        def scatter(o_ref, offset, index, carry):
+            here = pl.ds(pl.multiple_of(index * lines, lines), lines)
+            there = pl.ds(pl.multiple_of(offset + index * lines, lines), lines)
+            parts = fast_fourier([held[p, there, :] for p in range(count)], -1.0)
+            for p, part in enumerate(parts):
+                part = part * (1.0 / (count * depth))
+                part = jnp.where(step == 0, pltpu.roll(part, half, 1), part)
+                before = o_ref[p, 0, here, :].astype(jnp.float32)
+                o_ref[p, 0, here, :] = jnp.where(placed, before, part).astype(jnp.bfloat16)
+            return carry
+
+        offset = 0
+        for o_ref, size in zip(o_refs, sizes):
+            lax.fori_loop(0, size // lines, functools.partial(scatter, o_ref, offset), 0)
+            offset += size
+
+
+def channel_filter(pencils, bounds, packed):
+    count, digits, _, width = pencils[0].shape
+    sizes = [pencil.shape[2] for pencil in pencils]
+    depth = sum(sizes)
+    outer = jnp.arange(count, dtype=jnp.int32)
+    inner = jnp.arange(depth, dtype=jnp.int32)
+    cos_b, sin_b = rotations(inner, inner, depth)
+    tw_cos, tw_sin = rotations(outer, inner, count * depth)
+    signs = jnp.where(jnp.arange(width) < width // 2, 1.0, -1.0).astype(jnp.float32)
+    tw_cos = jnp.broadcast_to(tw_cos[:, :, None], (count, depth, width))
+    tw_sin = tw_sin[:, :, None] * signs
+    ahead = jnp.concatenate(split_table(jnp.concatenate([cos_b, sin_b], axis=1)), axis=0)
+    behind = jnp.concatenate(split_table(jnp.concatenate([cos_b, -sin_b], axis=1)), axis=0)
+    once = pl.Buffered(1)
+    flat = lambda s: (0, 0)
+    solid = lambda s: (0, 0, 0)
+    at = lambda s: (0, jnp.maximum(s - 1, 0), 0, 0)
+    blocks = [pl.BlockSpec((count, 1, size, width), at) for size in sizes]
+    return pl.pallas_call(
+        functools.partial(channel_kernel, sizes),
+        grid=(digits + 1,),
+        in_specs=[
+            pl.BlockSpec(memory_space=pltpu.SMEM),
+            pl.BlockSpec((1, 8, width), lambda s: (s, 0, 0)),
+            pl.BlockSpec(tw_cos.shape, solid, pipeline_mode=once),
+            pl.BlockSpec(tw_sin.shape, solid, pipeline_mode=once),
+            pl.BlockSpec(ahead.shape, flat, pipeline_mode=once),
+            pl.BlockSpec(behind.shape, flat, pipeline_mode=once),
+        ]
+        + blocks,
+        out_specs=blocks,
+        out_shape=[jax.ShapeDtypeStruct(pencil.shape, jnp.bfloat16) for pencil in pencils],
+        scratch_shapes=[pltpu.VMEM((count, depth, width), jnp.float32)],
+        compiler_params=pltpu.CompilerParams(vmem_limit_bytes=56 * 2**20),
+        name="channel_filter",
+    )(packed, bounds, tw_cos, tw_sin, ahead, behind, *pencils)
+
+
+def step_bounds(window, top):
+    digits = window.shape[1]
+    wide = jnp.concatenate([window, window], axis=2)
+    above = jnp.broadcast_to(top[:, None, None], (2, 1, wide.shape[2]))
+    bounds = jnp.concatenate([above, wide], axis=1).transpose(1, 0, 2)
+    return jnp.pad(bounds, ((0, 0), (0, 6), (0, 0)))
 
 
 EDGE = 16
@@ -335,40 +415,28 @@
     digits = TF // devices
     tiles = record * channel_ok.astype(jnp.bfloat16)[:, None]
     tiles = tiles.reshape(time_count, row_count, tile_time // TF, TF)
-    series = lax.all_to_all(tiles, "tm", split_axis=0, concat_axis=0)
+    first = (row_count // EDGE + 1) // 2 * EDGE
+    series = [
+        lax.all_to_all(part, "tm", split_axis=0, concat_axis=0)
+        for part in (tiles[:, :first], tiles[:, first:])
+    ]
     block_index = lax.axis_index("chan") * time_count + lax.axis_index("tm")
-    top_low = fan_bounds[0, NT // 2]
-    top_high = fan_bounds[1, NT // 2]
-    columns = digits * half
-    ordered = (
-        fan_bounds[:, : NT // 2].reshape(2, TF // 2, TF).transpose(0, 2, 1).reshape(2, NT // 2)
-    )
-    packed = (block_index == 0).astype(jnp.float32)
-    window = lax.dynamic_slice_in_dim(ordered, block_index * columns, columns, 1)
-    slot_index = jnp.arange(devices, dtype=jnp.int32)
-    spec = time_forward(series).reshape(devices, digits, row_count, TF)
-    pencil = lax.all_to_all(spec, ("chan", "tm"), split_axis=0, concat_axis=0)
-
-    def flat(part):
-        return part.transpose(0, 2, 1, 3).reshape(NC, columns)
-
-    def folded(part):
-        return part.reshape(devices, row_count, digits, half).transpose(0, 2, 1, 3)
-
-    filt_re, filt_im = channel_filter(
-        flat(pencil[..., :half]),
-        flat(pencil[..., half:]),
-        slot_index,
-        window[0],
-        window[1],
-        top_low,
-        top_high,
-        packed,
-    )
-    filt = jnp.concatenate([folded(filt_re), folded(filt_im)], axis=3)
-    back = lax.all_to_all(filt, ("chan", "tm"), split_axis=0, concat_axis=0)
-    rows = time_inverse(back.reshape(TF, row_count, TF), time_count)
-    rows = lax.all_to_all(rows, "tm", split_axis=0, concat_axis=0)
+    ordered = fan_bounds[:, : NT // 2].reshape(2, half, TF).transpose(0, 2, 1)
+    window = lax.dynamic_slice_in_dim(ordered, block_index * digits, digits, 1)
+    bounds = step_bounds(window, fan_bounds[:, NT // 2])
+    packed = (block_index == 0).astype(jnp.int32)[None]
+    everyone = ("chan", "tm")
+    pencils = []
+    for part in series:
+        spec = time_forward(part)
+        spec = spec.reshape(devices, digits, spec.shape[1], TF)
+        pencils.append(lax.all_to_all(spec, everyone, split_axis=0, concat_axis=0))
+    rows = []
+    for part in channel_filter(pencils, bounds, packed):
+        back = lax.all_to_all(part, everyone, split_axis=0, concat_axis=0)
+        lines = time_inverse(back.reshape(TF, back.shape[2], TF), time_count)
+        rows.append(lax.all_to_all(lines, "tm", split_axis=0, concat_axis=0))
+    rows = jnp.concatenate(rows, axis=1)
     return tensor_slowness(rows.reshape(tile_chan, tile_time))
 
 

time: 1800 us -> 1450 us (0.81)
  waiting for transfers between devices: 681 us -> 415 us
  matrix products: 241 us -> 0 us
  Pallas kernels: 285 us -> 486 us
  blocking collectives: 233 us -> 404 us
  local copies, waits for them, and re-layouts: 205 us -> 56 us
  other arithmetic: 103 us -> 32.3 us
    all_to_all x3 -> x5, waiting for transfers between devices: 673 us -> 405 us  [the longest x2 190 us: per_device(): pencils.append(lax.all_to_all(spec, everyone, split_axis=0, concat_axis=0))]
    dot_general x16 -> x0, matrix products: 241 us -> none  [contract(): jnp.einsum(pattern, left_arg, right_arg, precision=lax.Precision.HIGH, pr...]
    pallas_call x0 -> x1, Pallas kernels: none -> 199 us  [channel_filter(): pl.pallas_call(functools.partial(channel_kernel, sizes), grid=(digits + 1...]
    all_to_all x1 -> x3, blocking collectives: 233 us -> 404 us  [the longest x1 165 us: per_device(): back = lax.all_to_all(part, everyone, split_axis=0, concat_axis=0)]
    dot_general x4 -> x0, local copies, waits for them, and re-layouts: 48.1 us -> none  [contract(): jnp.einsum(pattern, left_arg, right_arg, precision=lax.Precision.HIGH, pr...]
    transpose x3 -> x0, local copies, waits for them, and re-layouts: 42 us -> none  [flat(): return part.transpose(0, 2, 1, 3).reshape(NC, columns)]
    sub x1 -> x0, other arithmetic: 36.5 us -> none  [channel_filter(): untwist_re = back_re * tw_cos - back_im * tw_sin]
    mul x2 -> x1, other arithmetic: 33.3 us -> 3.6 us  [channel_filter(): tw_sin = tw_sin[:, :, None] * signs]
  transfers between devices with their start and end apart: 7 -> 9, of which waited for: 6 -> 8; matrix products, arithmetic and copies ran while one was open for 0% -> 1% of each run, Pallas kernels for 0% -> 10%
where the time goes in v2:
time: 1450 us; the launch traced here: 1440 us
  Pallas kernels  486 us (34%)
  waiting for transfers between devices  415 us (29%)
  blocking collectives  404 us (28%)
  local copies, waits for them, and re-layouts  56 us (4%)
  starting transfers between devices  43.9 us (3%)
  other arithmetic  32.3 us (2%)
    pallas_call x1, Pallas kernels, channel_filter(): pl.pallas_call(functools.partial(channel_kernel, sizes), grid=(digits + 1...  199 us
    all_to_all x2, waiting for transfers between devices, per_device(): pencils.append(lax.all_to_all(spec, everyone, split_axis=0, concat_axis=0))  190 us
    all_to_all x1, blocking collectives, per_device(): back = lax.all_to_all(part, everyone, split_axis=0, concat_axis=0)  165 us
    pallas_call x1, Pallas kernels, tensor_slowness(): pl.pallas_call(tensor_kernel, grid=(tile_chan // rows,), in_specs=[pl.Blo...  144 us
    all_to_all x1, blocking collectives, per_device(): rows.append(lax.all_to_all(lines, 'tm', split_axis=0, concat_axis=0))  120 us
    all_to_all x1, blocking collectives, per_device(): lax.all_to_all(part, 'tm', split_axis=0, concat_axis=0)  119 us
    pallas_call x2, Pallas kernels, time_inverse(): pl.pallas_call(inverse_kernel, grid=(row_count // rows,), in_specs=[pl.Bl...  90.5 us
    all_to_all x1, waiting for transfers between devices, per_device(): lax.all_to_all(part, 'tm', split_axis=0, concat_axis=0)  82.6 us
  transfers between devices with their start and end apart: 9, of which 8 were waited for; matrix products, arithmetic and copies ran while one was open for 1% of the time, Pallas kernels for 10%

profile of v2, /device:TPU:19, one launch (start us, length us, event | category | flops | bytes accessed | tf_op | source)
XLA Modules:
  0.0 1437.7 jit_solution(4503569822792576438)
XLA Ops:
  0.0 0.7 convert_element_type.123
  0.7 10.0 multiply_bitcast_fusion
  10.7 11.6 copy.7
  22.3 9.9 fusion.39
  32.2 118.8 %all_to_all.40.x_ref = bf16[4,160,32,128]{3,2,1,0:T(8,128)(2,1)} all-to-all(bf16[4,160,32,128]{3,2,1,0:T(8,128)(2,1)} %get-tuple-element.14), channel_id=1, replica_groups=mesh['chan'=8,'tm'=4] {'tm'}, dimensions={0} | all-to-all | bytes 10485760 | tf_op jit(solution)/shard_map/all_to_all | solution.py:420
  150.9 7.2 all-to-all-start.2
  158.4 0.3 fusion.35
  159.1 26.1 %time_forward.2 = bf16[128,160,128]{2,1,0:T(8,128)(2,1)S(1)} custom-call(bf16[4,160,32,128]{3,2,1,0:T(8,128)(2,1)} %all_to_all.40.x_ref, bf16[256,256]{1,0:T(8,128)(2,1)S(1)} %pad_maximum_fusion.8.w_ref, f32[128,128]{1,0:T(8,128)S(1)} %get-tuple-element.42.tc_ref, f32[128,128]{1,0:T(8,128)S(1)} %get-tuple-element.41.ts_ref, ...), custom_call_target="tpu_custom_call" | custom-call | tf_op jit(solution)/shard_map/time_forward/pallas_call | solution.py:83
  185.3 2.3 copy-done.1
  187.6 82.6 %all-to-all-done.2.x_ref = bf16[4,160,32,128]{3,2,1,0:T(8,128)(2,1)} async-done(((bf16[4,160,32,128]{3,2,1,0:T(8,128)(2,1)}), bf16[4,160,32,128]{3,2,1,0:T(8,128)(2,1)}, u32[]{:S(2)}, u32[]{:S(2)}) %all-to-all-start.2) | async-done | bytes 5242912 | tf_op jit(solution)/shard_map/all_to_all | solution.py:420
  270.2 8.3 all-to-all-start.1
  278.5 26.2 %time_forward.3 = bf16[128,160,128]{2,1,0:T(8,128)(2,1)S(1)} custom-call(bf16[4,160,32,128]{3,2,1,0:T(8,128)(2,1)} %all-to-all-done.2.x_ref, bf16[256,256]{1,0:T(8,128)(2,1)S(1)} %pad_maximum_fusion.8.w_ref, f32[128,128]{1,0:T(8,128)S(1)} %get-tuple-element.42.tc_ref, f32[128,128]{1,0:T(8,128)S(1)} %get-tuple-element.41.ts_ref, ...), custom_call_target="tpu_custom_call" | custom-call | tf_op jit(solution)/shard_map/time_forward/pallas_call | solution.py:83
  304.7 2.3 copy-done
  307.0 86.9 %all-to-all-done.1.refs_0_ = bf16[32,4,160,128]{3,2,1,0:T(8,128)(2,1)} async-done(((bf16[32,4,160,128]{3,2,1,0:T(8,128)(2,1)}), bf16[32,4,160,128]{3,2,1,0:T(8,128)(2,1)}, u32[]{:S(2)}, u32[]{:S(2)}) %all-to-all-start.1) | async-done | bytes 5242912 | tf_op jit(solution)/shard_map/all_to_all | solution.py:433
  393.9 5.9 all-to-all-start.3
  400.3 0.6 pad.4.bound_ref
  401.3 1.9 fusion.9
  403.2 1.9 fusion.7
  405.1 1.9 fusion.6
  406.9 0.4 reduce-precision_convert_fusion
  407.3 1.3 pad_maximum_fusion.3
  408.6 3.6 broadcast_multiply_fusion.ts_ref
  412.2 102.9 %all-to-all-done.3.refs_1_ = bf16[32,4,160,128]{3,2,1,0:T(8,128)(2,1)} async-done(((bf16[32,4,160,128]{3,2,1,0:T(8,128)(2,1)}), bf16[32,4,160,128]{3,2,1,0:T(8,128)(2,1)}, u32[]{:S(2)}, u32[]{:S(2)}) %all-to-all-start.3) | async-done | bytes 5242912 | tf_op jit(solution)/shard_map/all_to_all | solution.py:433
  515.1 3.5 broadcast_in_dim.22.tc_ref
  518.6 199.5 %channel_filter.1 = (bf16[32,4,160,128]{3,2,1,0:T(8,128)(2,1)}, bf16[32,4,160,128]{3,2,1,0:T(8,128)(2,1)}) custom-call(s32[1]{0:T(128)} %bitcast.2.flag_ref, s32[5,8,128]{2,1,0:T(8,128)} %pad.4.bound_ref, f32[32,320,128]{2,1,0:T(8,128)} %broadcast_in_dim.22.tc_ref, f32[32,320,128]{2,1,0:T(8,128)} %broadcast_multiply_fusion.ts_ref, ...), custom_call_target="tpu_custom_call" | custom-call | tf_op jit(solution)/shard_map/channel_filter/pallas_call | solution.py:284
  718.0 165.4 %all_to_all.41 = bf16[32,4,160,128]{3,2,1,0:T(8,128)(2,1)} all-to-all(bf16[32,4,160,128]{3,2,1,0:T(8,128)(2,1)} %get-tuple-element.8), channel_id=1, replica_groups=mesh['chan'=8,'tm'=4] {'chan','tm'}, dimensions={0} | all-to-all | bytes 10485760 | tf_op jit(solution)/shard_map/all_to_all | solution.py:436
  883.4 4.8 all-to-all-start.4
  888.3 0.3 broadcast_multiply_fusion.1
  888.7 45.3 %time_inverse.3 = bf16[4,160,32,128]{3,2,1,0:T(8,128)(2,1)S(1)} custom-call(bf16[128,160,128]{2,1,0:T(8,128)(2,1)} %bitcast.34, bf16[256,256]{1,0:T(8,128)(2,1)S(1)} %pad_maximum_fusion.10.b_ref, f32[128,128]{1,0:T(8,128)S(1)} %get-tuple-element.44.tc_ref, f32[128,128]{1,0:T(8,128)S(1)} %get-tuple-element.43.ts_ref, ...), custom_call_target="tpu_custom_call" | custom-call | tf_op jit(solution)/shard_map/time_inverse/pallas_call | solution.py:150
  934.0 2.3 copy-done.2
  936.3 67.5 %all-to-all-done.4 = bf16[32,4,160,128]{3,2,1,0:T(8,128)(2,1)} async-done(((bf16[32,4,160,128]{3,2,1,0:T(8,128)(2,1)}), bf16[32,4,160,128]{3,2,1,0:T(8,128)(2,1)}, u32[]{:S(2)}, u32[]{:S(2)}) %all-to-all-start.4) | async-done | bytes 5242912 | tf_op jit(solution)/shard_map/all_to_all | solution.py:436
  1003.8 5.6 all-to-all-start.7
  1009.4 45.3 %time_inverse.2 = bf16[4,160,32,128]{3,2,1,0:T(8,128)(2,1)S(1)} custom-call(bf16[128,160,128]{2,1,0:T(8,128)(2,1)} %bitcast.7.p_ref, bf16[256,256]{1,0:T(8,128)(2,1)S(1)} %pad_maximum_fusion.10.b_ref, f32[128,128]{1,0:T(8,128)S(1)} %get-tuple-element.44.tc_ref, f32[128,128]{1,0:T(8,128)S(1)} %get-tuple-element.43.ts_ref, ...), custom_call_target="tpu_custom_call" | custom-call | tf_op jit(solution)/shard_map/time_inverse/pallas_call | solution.py:150
  1054.7 2.4 copy-done.3
  1057.0 65.0 %all-to-all-done.7 = bf16[4,160,32,128]{3,2,1,0:T(8,128)(2,1)} async-done(((bf16[4,160,32,128]{3,2,1,0:T(8,128)(2,1)}), bf16[4,160,32,128]{3,2,1,0:T(8,128)(2,1)}, u32[]{:S(2)}, u32[]{:S(2)}) %all-to-all-start.7) | async-done | bytes 5242912 | tf_op jit(solution)/shard_map/all_to_all | solution.py:438
  1122.0 119.8 %all_to_all.42 = bf16[4,160,32,128]{3,2,1,0:T(8,128)(2,1)S(1)} all-to-all(bf16[4,160,32,128]{3,2,1,0:T(8,128)(2,1)} %copy-done.3), channel_id=1, replica_groups=mesh['chan'=8,'tm'=4] {'tm'}, dimensions={0} | all-to-all | bytes 10485760 | tf_op jit(solution)/shard_map/all_to_all | solution.py:438
  1241.8 8.8 pad_maximum_fusion
  1250.5 18.6 %copy.11 = bf16[160,8,32,128]{3,1,2,0:T(8,128)(2,1)} copy(bf16[160,8,32,128]{3,2,1,0:T(8,128)(2,1)} %bitcast.33) | data formatting | bytes 20971520
  1269.1 1.0 fusion.38
  1270.1 3.4 collective-permute-start.1
  1273.5 1.1 fusion.37
  1274.7 3.0 collective-permute-start
  1277.8 1.9 collective-permute-done.head_ref
  1279.7 3.8 collective-permute-start.2
  1283.5 1.9 collective-permute-start.3
  1285.5 4.1 collective-permute-done.2.left_ref
  1289.7 3.9 collective-permute-done.3.right_ref
  1293.5 143.7 %tensor_slowness.1 = f32[1280,4096]{1,0:T(8,128)} custom-call(s32[2]{0:T(128)S(1)} %pad_add_fusion.where_ref, bf16[1280,4096]{1,0:T(8,128)(2,1)} %bitcast.29, bf16[1280,4096]{1,0:T(8,128)(2,1)} %bitcast.30, bf16[1280,4096]{1,0:T(8,128)(2,1)} %bitcast.31, bf16[16,4096]{1,0:T(8,128)(2,1)S(1)} %collective-permute-done.head_ref, ...), custom_call_target="tpu_custom_call" | custom-call | tf_op jit(solution)/shard_map/tensor_slowness/pallas_call | solution.py:388
  (35 shorter events, 1.8 us)
Async XLA Ops:
  150.9 119.3 %all-to-all-start.2 = ((bf16[4,160,32,128]{3,2,1,0:T(8,128)(2,1)}), bf16[4,160,32,128]{3,2,1,0:T(8,128)(2,1)}, u32[]{:S(2)}, u32[]{:S(2)}) async-start(bf16[4,160,32,128]{3,2,1,0:T(8,128)(2,1)} %get-tuple-element.13), calls=%async_computation.2 | async-start | bytes 10485760 | tf_op jit(solution)/shard_map/all_to_all | solution.py:420
  185.3 2.3 copy-start.1
  270.2 123.7 %all-to-all-start.1 = ((bf16[32,4,160,128]{3,2,1,0:T(8,128)(2,1)}), bf16[32,4,160,128]{3,2,1,0:T(8,128)(2,1)}, u32[]{:S(2)}, u32[]{:S(2)}) async-start(bf16[32,4,160,128]{3,2,1,0:T(8,128)(2,1)} %bitcast.26), calls=%async_computation.1 | async-start | bytes 10485760 | tf_op jit(solution)/shard_map/all_to_all | solution.py:433
  304.6 2.4 copy-start
  393.9 5.9 copy-start.4
  393.9 121.2 %all-to-all-start.3 = ((bf16[32,4,160,128]{3,2,1,0:T(8,128)(2,1)}), bf16[32,4,160,128]{3,2,1,0:T(8,128)(2,1)}, u32[]{:S(2)}, u32[]{:S(2)}) async-start(bf16[32,4,160,128]{3,2,1,0:T(8,128)(2,1)} %bitcast.25), calls=%async_computation.3 | async-start | bytes 10485760 | tf_op jit(solution)/shard_map/all_to_all | solution.py:433
  883.4 120.3 %all-to-all-start.4 = ((bf16[32,4,160,128]{3,2,1,0:T(8,128)(2,1)}), bf16[32,4,160,128]{3,2,1,0:T(8,128)(2,1)}, u32[]{:S(2)}, u32[]{:S(2)}) async-start(bf16[32,4,160,128]{3,2,1,0:T(8,128)(2,1)} %get-tuple-element.7), calls=%async_computation.4 | async-start | bytes 10485760 | tf_op jit(solution)/shard_map/all_to_all | solution.py:436
  933.9 2.4 copy-start.2
  1003.8 118.2 %all-to-all-start.7 = ((bf16[4,160,32,128]{3,2,1,0:T(8,128)(2,1)}), bf16[4,160,32,128]{3,2,1,0:T(8,128)(2,1)}, u32[]{:S(2)}, u32[]{:S(2)}) async-start(bf16[4,160,32,128]{3,2,1,0:T(8,128)(2,1)} %copy-done.2), calls=%async_computation.7 | async-start | bytes 10485760 | tf_op jit(solution)/shard_map/all_to_all | solution.py:438
  1054.7 2.4 copy-start.3
  1270.1 7.6 collective-permute-start.1
  1274.7 5.0 collective-permute-start
  1279.7 10.0 collective-permute-start.2
  1283.5 10.0 collective-permute-start.3
